TPU v7x, 128 devices: a whole 4x4x4 slice. The times are simulated.
128 devices in a mesh: hilbert: 128 (over x, z, y, core).
Axes of the slice: x: 4, y: 4, z: 4, core: 2. Of those that a mesh axis runs over, the one named last changes fastest.
Arguments:
- positions: float32 [16384, 3, 256], P('hilbert'), may hold values from 0.5 to 7.5
- masses: float32 [16384, 256], P('hilbert'), may hold values from 0.5 to 4.5
- block_owner: int32 [16384, 1], P('hilbert'), may hold values from 0 to 127, as said below
- block_oct: int32 [16384], P('hilbert'), may hold values from 0 to 63
- face_owner: int32 [8192, 6, 1], P('hilbert'), may hold values from 0 to 127, as said below
- face_oct: int32 [8192, 6], P('hilbert'), may hold values from 0 to 63
- face_coarse: int32 [8192, 6], P('hilbert'), may hold values 0 or 1
- face_quadrant: int32 [8192, 6], P('hilbert'), may hold values from 0 to 3
Outputs:
- potential: float32 [8192, 512], P('hilbert')
- accel: float32 [16384, 3, 256], P('hilbert')
Inputs may be any that keep to these rules, and one draw needn't show every extreme that they name: `block_owner`: each block's owner is its own device, a device at most 4 positions away, or the device 128 / 2 positions away counted round; among the 128 blocks of one device at most 4 have any one other owner, and some other owner has exactly 4. `face_owner`: each face's neighbour owner is the face's own device, a device at most 4 positions away, or the device 128 / 2 positions away counted round; among the 384 faces of one device's octs at most 12 have a neighbour of any one other owner, and some other owner has exactly 12.
All inputs are finite; a program needn't handle non-finite values. No bound on the sum of `face_coarse` on one device may be relied on, other than what follows from the above.
Results may differ from a plain program's by a relative error of at most 0.002.
Values may be sent and summed in bfloat16 or wider, within the bound.
A program may use at most 64 MiB of HBM per device.

v0:
```python
import math

import jax
import jax.numpy as jnp
from jax import lax
from jax.sharding import PartitionSpec as P

EDGE = 8
SWEEPS = 8


coupling = 0.25
group_rows = 128
highest_level = lax.Precision.HIGHEST


def cloud_weights(positions):
    centres = jnp.arange(EDGE).astype(positions.dtype) + 0.5
    return jnp.maximum(0.0, 1.0 - jnp.abs(positions[:, :, None, :] - centres[None, None, :, None]))


def cross_weights(weight_factors):
    row_count = weight_factors.shape[0]
    return (weight_factors[:, 1, :, None, :] * weight_factors[:, 2, None, :, :]).reshape(
        row_count, EDGE * EDGE, weight_factors.shape[3]
    )


def deposit_block(positions, masses):
    weight_factors = cloud_weights(positions)
    crossed_faces = cross_weights(weight_factors)
    weighted_x = weight_factors[:, 0] * masses[:, None, :]
    mesh_grid = jnp.einsum("mle,mbe->mlb", weighted_x, crossed_faces, precision=highest_level)
    return mesh_grid.reshape(positions.shape[0], EDGE**3)


def interpolate_block(positions, field):
    weight_factors = cloud_weights(positions)
    crossed_faces = cross_weights(weight_factors)
    value_rows = field.astype(jnp.float32).reshape(positions.shape[0], 3, EDGE, EDGE * EDGE)
    partial_field_value = jnp.einsum(
        "enlh,ehi->enli", value_rows, crossed_faces, precision=highest_level
    )
    return jnp.sum(partial_field_value * weight_factors[:, 0][:, None, :, :], axis=2)


def by_groups(action, arrays):
    row_count = arrays[0].shape[0]
    group_size = math.gcd(row_count, group_rows)
    shaped = tuple(
        (
            source_array.reshape((row_count // group_size, group_size) + source_array.shape[1:])
            for source_array in arrays
        )
    )
    results = lax.map(lambda members: action(*members), shaped)
    return results.reshape((row_count,) + results.shape[2:])


def cell_coords():
    cells = jnp.arange(EDGE**3, dtype=jnp.int32)
    return (cells // (EDGE * EDGE), cells // EDGE % EDGE, cells % EDGE)


def face_matrix():
    xs, ys, zs = cell_coords()
    coords = (xs, xs, ys, ys, zs, zs)
    spots = (
        ys * EDGE + zs,
        ys * EDGE + zs,
        xs * EDGE + zs,
        xs * EDGE + zs,
        xs * EDGE + ys,
        xs * EDGE + ys,
    )
    slots = jnp.arange(EDGE * EDGE, dtype=jnp.int32)
    columns = []
    for face in range(6):
        bound = 0 if face % 2 == 0 else EDGE - 1
        picked = (coords[face] == bound)[:, None] & (spots[face][:, None] == slots[None, :])
        columns.append(picked.astype(jnp.float32))
    return jnp.concatenate(columns, axis=1)


def face_layers(potential, table):
    layers = jnp.dot(potential, table, precision=highest_level, preferred_element_type=jnp.float32)
    return layers.reshape(-1, EDGE * EDGE)


def inner_pairs(potential):
    row_count = potential.shape[0]
    xs, ys, zs = cell_coords()
    result = []
    for stride, coord in ((EDGE * EDGE, xs), (EDGE, ys), (1, zs)):
        padding = jnp.zeros((row_count, stride), jnp.float32)
        upper = jnp.concatenate([potential[:, stride:], padding], axis=1)
        lower = jnp.concatenate([padding, potential[:, : EDGE**3 - stride]], axis=1)
        upper = jnp.where((coord < EDGE - 1)[None, :], upper, 0.0)
        lower = jnp.where((coord > 0)[None, :], lower, 0.0)
        result.append((upper, lower))
    return result


def placed_face(ghost_flat, table, face):
    width = EDGE * EDGE
    return jnp.dot(
        ghost_flat[:, face * width : (face + 1) * width],
        table[:, face * width : (face + 1) * width].T,
        precision=highest_level,
        preferred_element_type=jnp.float32,
    )


def jacobi_sweep(potential, ghost_flat, source, table):
    pairs = inner_pairs(potential)
    placed = jnp.dot(
        ghost_flat, table.T, precision=highest_level, preferred_element_type=jnp.float32
    )
    summed_partials = (
        pairs[0][0] + pairs[0][1] + pairs[1][0] + pairs[1][1] + pairs[2][0] + pairs[2][1] + placed
    )
    return (summed_partials - coupling * source) / 6.0


def force_field(potential, ghost_flat, table):
    pairs = inner_pairs(potential)
    parts = []
    for dim_id in range(3):
        upper = pairs[dim_id][0] + placed_face(ghost_flat, table, 2 * dim_id + 1)
        lower = pairs[dim_id][1] + placed_face(ghost_flat, table, 2 * dim_id)
        parts.append(-0.5 * (upper - lower))
    return jnp.stack(parts, axis=1).astype(jnp.bfloat16)


def refine_table():
    cell_ids = jnp.arange(EDGE * EDGE)
    across = cell_ids // EDGE
    along = cell_ids % EDGE
    quarters = jnp.arange(4)
    half_edge = EDGE // 2
    first_idx = quarters[:, None] // 2 * half_edge + across[None, :] // 2
    second_idx = quarters[:, None] % 2 * half_edge + along[None, :] // 2
    return first_idx * EDGE + second_idx


def resolve_ghosts(layers, coarser, quadrant):
    table = refine_table()
    refined = jnp.take_along_axis(layers, table[quadrant], axis=1)
    return jnp.where(coarser[:, None] == 1, refined, layers)


def lane_codes(owner_ids, my_index, peer_count):
    return (jnp.where(owner_ids == my_index, -1, owner_ids), peer_count)


def lane_places(lane_ids, lane_count, capacity):
    matches = (lane_ids[:, None] == jnp.arange(lane_count, dtype=jnp.int32)[None, :]).astype(
        jnp.int32
    )
    before = jnp.cumsum(matches, axis=0) - matches
    places = lane_ids * capacity + jnp.sum(before * matches, axis=1)
    return jnp.where(lane_ids >= 0, places, lane_count * capacity)


def partials_to_owner(buffers):
    return lax.all_to_all(buffers, "hilbert", split_axis=0, concat_axis=0, tiled=True)


def field_to_blocks(value_rows):
    return lax.all_to_all(value_rows, "hilbert", split_axis=0, concat_axis=0, tiled=True)


def requests_to_owner(asking):
    return lax.all_to_all(asking, "hilbert", split_axis=0, concat_axis=0, tiled=True)


def faces_to_asker(reply, capacity, lane_count):
    wide = reply.reshape(lane_count, capacity * EDGE * EDGE)
    return (
        lax.all_to_all(
            wide.astype(jnp.bfloat16), "hilbert", split_axis=0, concat_axis=0, tiled=True
        )
        .astype(wide.dtype)
        .reshape(lane_count * capacity, EDGE * EDGE)
    )


def collect_octs(deposits, slot_octs, oct_count):
    matches = (jnp.arange(oct_count, dtype=jnp.int32)[:, None] == slot_octs[None, :]).astype(
        jnp.float32
    )
    return jnp.dot(matches, deposits, precision=highest_level, preferred_element_type=jnp.float32)


def on_device(
    positions, masses, block_owner, block_oct, face_owner, face_oct, face_coarse, face_quadrant
):
    peer_count = lax.axis_size("hilbert")
    my_index = lax.axis_index("hilbert")
    block_count = positions.shape[0]
    oct_count = face_oct.shape[0]
    block_cap = block_count // 32
    face_cap = 3 * oct_count // 16
    owner_ids = block_owner[:, 0]
    at_home = owner_ids == my_index
    home_octs = jnp.where(at_home, block_oct, -1)
    block_lane, lane_count = lane_codes(owner_ids, my_index, peer_count)
    block_place = lane_places(block_lane, lane_count, block_cap)
    slot_count = lane_count * block_cap
    block_read = jnp.minimum(block_place, slot_count - 1)
    slot_octs = jnp.full((slot_count,), -1, jnp.int32).at[block_place].set(block_oct, mode="drop")
    deposits = by_groups(deposit_block, (positions, masses))
    send_dep = (
        jnp.zeros((slot_count, EDGE**3), jnp.float32).at[block_place].set(deposits, mode="drop")
    )
    got_dep, got_octs = partials_to_owner((send_dep, slot_octs))
    density = collect_octs(
        jnp.concatenate([deposits, got_dep], axis=0),
        jnp.concatenate([home_octs, got_octs], axis=0),
        oct_count,
    )
    mass_sum = lax.psum(jnp.sum(density), "hilbert")
    mean_density = mass_sum / (peer_count * oct_count * EDGE**3)
    source = density - mean_density
    table = face_matrix()
    opposite = jnp.array([1, 0, 3, 2, 5, 4], dtype=jnp.int32)
    wanted_cells = (face_oct * 6 + opposite[None, :]).reshape(-1)
    face_owners = face_owner.reshape(-1)
    face_home = face_owners == my_index
    face_lane, face_lanes = lane_codes(face_owners, my_index, peer_count)
    face_place = lane_places(face_lane, face_lanes, face_cap)
    face_read = jnp.minimum(face_place, face_lanes * face_cap - 1)
    asking = (
        jnp.full((face_lanes * face_cap,), -1, jnp.int32)
        .at[face_place]
        .set(wanted_cells, mode="drop")
    )
    asked = jnp.maximum(requests_to_owner(asking), 0)
    coarser = face_coarse.reshape(-1)
    quadrant = face_quadrant.reshape(-1)

    def ghosts(potential):
        own_faces = face_layers(potential, table)
        returned = faces_to_asker(own_faces[asked], face_cap, face_lanes)
        layers = jnp.where(face_home[:, None], own_faces[wanted_cells], returned[face_read])
        return resolve_ghosts(layers, coarser, quadrant).reshape(oct_count, 6 * EDGE * EDGE)

    potential = jnp.zeros((oct_count, EDGE**3), jnp.float32)
    for sweep_round in range(SWEEPS):
        if sweep_round == 0:
            ghost = jnp.zeros((oct_count, 6 * EDGE * EDGE), jnp.float32)
        else:
            ghost = ghosts(potential)
        potential = jacobi_sweep(potential, ghost, source, table)
    field = force_field(potential, ghosts(potential), table)
    returned_field = field_to_blocks(field[jnp.maximum(got_octs, 0)])
    block_field = jnp.where(
        at_home[:, None, None], field[jnp.maximum(home_octs, 0)], returned_field[block_read]
    )
    accel = by_groups(interpolate_block, (positions, block_field))
    return (potential, accel)


def solution(mesh):
    placed = (
        P("hilbert", None, None),
        P("hilbert", None),
        P("hilbert", None),
        P("hilbert"),
        P("hilbert", None, None),
        P("hilbert", None),
        P("hilbert", None),
        P("hilbert", None),
    )
    return jax.shard_map(
        on_device,
        mesh=mesh,
        in_specs=placed,
        out_specs=(P("hilbert", None), P("hilbert", None, None)),
        check_vma=False,
    )
```

profile of v0, /device:TPU:1, one launch (start us, length us, event | category | flops | bytes accessed | tf_op | source)
XLA Modules:
  0.0 1668.2 jit_solution(15136030234169419383)
XLA Ops:
  1.7 1.3 fusion.91
  4.8 12.0 all-to-all-start
  21.0 1.6 subtract_maximum_fusion
  22.6 1.8 slice_bitcast_fusion.2
  27.7 1.2 broadcast_compare_fusion
  28.9 9.1 fusion
  39.9 3.1 scatter_custom_fusion.2
  43.7 9.8 all-to-all-start.2
  53.5 1.2 copy.47
  54.9 1.4 scatter_custom_fusion.1
  56.3 1.3 all_to_all.60
  57.5 5.3 all-to-all-done.2
  62.9 4.6 all-to-all-start.1
  69.5 1.8 maximum_reduce_fusion
  72.5 14.1 all-to-all-done.1
  86.9 1.2 fusion.125
  88.2 63.0 %psum.7 = f32[]{:T(128)} all-reduce(f32[]{:T(128)} %get-tuple-element.97), channel_id=1, replica_groups=mesh['hilbert'=128] {'hilbert'}, use_global_device_ids=true, to_apply=%region_5.6 | all-reduce | flops 1 | bytes 8 | tf_op jit(solution)/shard_map/psum | solution.py:222
  153.0 2.6 gather_fusion.1
  156.4 1.8 reduce.37
  158.9 4.9 all-to-all-start.3
  163.8 1.1 gather_fusion
  165.0 9.0 all-to-all-done.3
  175.5 1.1 gather_fusion.2
  176.8 157.6 %gather_fusion.28 = f32[24576]{0:T(1024)S(1)} fusion(f32[384,64]{1,0:T(8,128)S(1)} %broadcast_select_fusion.8, s32[24576]{0:T(1024)S(1)} %reshape.1124), kind=kCustom, calls=%fused_computation.clone | custom fusion | bytes 393216 | tf_op jit(solution)/shard_map/jit(take_along_axis)/gather | solution.py:148
  335.6 2.6 gather_fusion.5
  339.8 1.8 reduce.38
  342.4 4.5 all-to-all-start.4
  346.9 10.3 all-to-all-done.4
  359.9 157.6 %gather_fusion.29 = f32[24576]{0:T(1024)S(1)} fusion(f32[384,64]{1,0:T(8,128)S(1)} %broadcast_select_fusion.7, s32[24576]{0:T(1024)S(1)} %reshape.1124), kind=kCustom, calls=%fused_computation.1.clone | custom fusion | bytes 393216 | tf_op jit(solution)/shard_map/jit(take_along_axis)/gather | solution.py:148
  518.8 2.6 gather_fusion.8
  522.9 1.8 reduce.39
  525.5 4.5 all-to-all-start.5
  530.0 10.3 all-to-all-done.5
  543.1 157.6 %gather_fusion.30 = f32[24576]{0:T(1024)S(1)} fusion(f32[384,64]{1,0:T(8,128)S(1)} %broadcast_select_fusion.6, s32[24576]{0:T(1024)S(1)} %reshape.1124), kind=kCustom, calls=%fused_computation.2.clone | custom fusion | bytes 393216 | tf_op jit(solution)/shard_map/jit(take_along_axis)/gather | solution.py:148
  701.9 2.6 gather_fusion.11
  706.1 1.8 reduce.40
  708.6 4.5 all-to-all-start.6
  713.2 10.3 all-to-all-done.6
  726.2 157.6 %gather_fusion.31 = f32[24576]{0:T(1024)S(1)} fusion(f32[384,64]{1,0:T(8,128)S(1)} %broadcast_select_fusion.5, s32[24576]{0:T(1024)S(1)} %reshape.1124), kind=kCustom, calls=%fused_computation.3.clone | custom fusion | bytes 393216 | tf_op jit(solution)/shard_map/jit(take_along_axis)/gather | solution.py:148
  885.0 2.6 gather_fusion.14
  887.7 1.1 gather_fusion.13
  889.2 1.8 reduce.41
  891.7 4.6 all-to-all-start.7
  896.4 10.4 all-to-all-done.7
  909.5 157.6 %gather_fusion.32 = f32[24576]{0:T(1024)S(1)} fusion(f32[384,64]{1,0:T(8,128)S(1)} %broadcast_select_fusion.4, s32[24576]{0:T(1024)S(1)} %reshape.1124), kind=kCustom, calls=%fused_computation.4.clone | custom fusion | bytes 393216 | tf_op jit(solution)/shard_map/jit(take_along_axis)/gather | solution.py:148
  1068.4 2.6 gather_fusion.17
  1072.6 1.8 reduce.42
  1075.1 4.5 all-to-all-start.8
  1079.7 10.3 all-to-all-done.8
  1092.6 157.6 %gather_fusion.33 = f32[24576]{0:T(1024)S(1)} fusion(f32[384,64]{1,0:T(8,128)S(1)} %broadcast_select_fusion.3, s32[24576]{0:T(1024)S(1)} %reshape.1124), kind=kCustom, calls=%fused_computation.5.clone | custom fusion | bytes 393216 | tf_op jit(solution)/shard_map/jit(take_along_axis)/gather | solution.py:148
  1251.5 2.6 gather_fusion.20
  1255.7 1.8 reduce.43
  1258.2 4.5 all-to-all-start.9
  1262.8 10.3 all-to-all-done.9
  1275.8 157.6 %gather_fusion.34 = f32[24576]{0:T(1024)S(1)} fusion(f32[384,64]{1,0:T(8,128)S(1)} %broadcast_select_fusion.2, s32[24576]{0:T(1024)S(1)} %reshape.1124), kind=kCustom, calls=%fused_computation.6.clone | custom fusion | bytes 393216 | tf_op jit(solution)/shard_map/jit(take_along_axis)/gather | solution.py:148
  1434.6 2.6 gather_fusion.23
  1438.8 1.8 reduce.44
  1441.4 4.8 all-to-all-start.10
  1446.3 10.2 all-to-all-done.10
  1459.2 157.6 %gather_fusion.35 = f32[24576]{0:T(1024)S(1)} fusion(f32[384,64]{1,0:T(8,128)S(1)} %broadcast_select_fusion.1, s32[24576]{0:T(1024)S(1)} %reshape.1124), kind=kCustom, calls=%fused_computation.7.clone | custom fusion | bytes 393216 | tf_op jit(solution)/shard_map/jit(take_along_axis)/gather | solution.py:148
  1620.1 3.8 gather_fusion.26
  1623.9 4.8 all-to-all-start.11
  1630.2 28.8 %all-to-all-done.11 = bf16[512,3,512]{2,1,0:T(4,128)(2,1)S(1)} async-done(((bf16[512,3,512]{2,1,0:T(4,128)(2,1)}), bf16[512,3,512]{2,1,0:T(4,128)(2,1)S(1)}, u32[]{:S(2)}, u32[]{:S(2)}) %all-to-all-start.11) | async-done | bytes 1572896 | tf_op jit(solution)/shard_map/all_to_all | solution.py:170
  1661.3 5.8 multiply_reduce_fusion
  (287 shorter events, 70.8 us)
Async XLA Ops:
  3.0 16.2 copy-start.33
  4.8 38.8 %all-to-all-start = ((s32[128,4,1]{1,2,0:T(1,128)}), s32[128,4,1]{1,2,0:T(1,128)}, u32[]{:S(2)}, u32[]{:S(2)}) async-start(s32[128,4,1]{1,2,0:T(1,128)} %bitcast.4), calls=%async_computation | async-start | bytes 131072 | tf_op jit(solution)/shard_map/all_to_all | solution.py:166
  16.8 21.2 %copy-start.3 = (s32[512]{0:T(512)}, s32[512]{0:T(512)S(1)}, u32[]{:S(2)}) copy-start(s32[512]{0:T(512)S(1)} %fusion.81) | copy-start | bytes 6148
  20.8 4.0 copy-start.9
  22.6 2.3 copy-start.14
  22.6 2.3 copy-start.31
  22.6 3.5 copy-start.12
  25.0 1.4 copy-start.2
  27.5 10.5 copy-start.15
  27.5 10.5 copy-start.19
  27.5 10.8 copy-start.5
  27.6 10.8 copy-start.17
  27.6 10.8 copy-start.23
  27.6 11.1 copy-start.7
  27.6 11.1 copy-start.21
  27.6 11.1 copy-start.25
  43.7 19.2 %all-to-all-start.2 = ((s32[128,12,1]{1,2,0:T(1,128)}), s32[128,12,1]{1,2,0:T(1,128)S(1)}, u32[]{:S(2)}, u32[]{:S(2)}) async-start(s32[128,12,1]{1,2,0:T(1,128)} %bitcast.13), calls=%async_computation.2 | async-start | bytes 131072 | tf_op jit(solution)/shard_map/all_to_all | solution.py:174
  54.7 12.9 copy-start.13
  54.8 13.6 copy-start.29
  54.8 13.6 copy-start.32
  54.9 14.1 copy-start.10
  62.9 23.7 %all-to-all-start.1 = ((f32[128,4,512]{2,1,0:T(4,128)}), f32[128,4,512]{2,1,0:T(4,128)S(1)}, u32[]{:S(2)}, u32[]{:S(2)}) async-start(f32[128,4,512]{2,1,0:T(4,128)} %all_to_all.60), calls=%async_computation.1 | async-start | bytes 2097152 | tf_op jit(solution)/shard_map/all_to_all | solution.py:166
  158.9 15.2 all-to-all-start.3
  342.4 14.8 all-to-all-start.4
  525.5 14.9 all-to-all-start.5
  708.6 14.9 all-to-all-start.6
  891.7 15.1 all-to-all-start.7
  1075.1 14.9 all-to-all-start.8
  1258.2 14.9 all-to-all-start.9
  1434.2 12.0 copy-start
  1441.4 15.1 all-to-all-start.10
  1459.1 158.0 %copy-start.8 = (s32[512]{0:T(512)S(1)}, s32[512]{0:T(512)}, u32[]{:S(2)}) copy-start(s32[512]{0:T(512)} %fusion.70) | copy-start | bytes 6148
  1459.1 158.0 %copy-start.26 = (pred[512]{0:T(512)(128)(4,1)S(1)}, pred[512]{0:T(512)(128)(4,1)}, u32[]{:S(2)}) copy-start(pred[512]{0:T(512)(128)(4,1)} %get-tuple-element.99) | copy-start | bytes 1540
  1459.2 158.4 %copy-start.6 = (s32[512]{0:T(512)S(1)}, s32[512]{0:T(512)}, u32[]{:S(2)}) copy-start(s32[512]{0:T(512)} %fusion.69) | copy-start | bytes 6148
  1459.2 158.4 %copy-start.24 = (pred[512]{0:T(512)(128)(4,1)S(1)}, pred[512]{0:T(512)(128)(4,1)}, u32[]{:S(2)}) copy-start(pred[512]{0:T(512)(128)(4,1)} %get-tuple-element.101) | copy-start | bytes 1540
  1459.2 158.9 %copy-start.4 = (s32[512]{0:T(512)S(1)}, s32[512]{0:T(512)}, u32[]{:S(2)}) copy-start(s32[512]{0:T(512)} %copy-done.3) | copy-start | bytes 6148
  1459.2 158.9 %copy-start.20 = (pred[512]{0:T(512)(128)(4,1)S(1)}, pred[512]{0:T(512)(128)(4,1)}, u32[]{:S(2)}) copy-start(pred[512]{0:T(512)(128)(4,1)} %get-tuple-element.103) | copy-start | bytes 1540
  1459.2 159.3 %copy-start.22 = (pred[512]{0:T(512)(128)(4,1)S(1)}, pred[512]{0:T(512)(128)(4,1)}, u32[]{:S(2)}) copy-start(pred[512]{0:T(512)(128)(4,1)} %get-tuple-element.100) | copy-start | bytes 1540
  1459.2 159.8 %copy-start.18 = (pred[512]{0:T(512)(128)(4,1)S(1)}, pred[512]{0:T(512)(128)(4,1)}, u32[]{:S(2)}) copy-start(pred[512]{0:T(512)(128)(4,1)} %get-tuple-element.102) | copy-start | bytes 1540
  1459.2 160.2 %copy-start.16 = (pred[512]{0:T(512)(128)(4,1)S(1)}, pred[512]{0:T(512)(128)(4,1)}, u32[]{:S(2)}) copy-start(pred[512]{0:T(512)(128)(4,1)} %get-tuple-element.104) | copy-start | bytes 1540
  1616.8 3.3 copy-start.11
  1623.9 4.8 copy-start.28
  1623.9 4.9 copy-start.30
  1623.9 36.5 %copy-start.27 = (pred[128]{0:T(512)(128)(4,1)S(1)}, pred[128]{0:T(512)(128)(4,1)}, u32[]{:S(2)}) copy-start(pred[128]{0:T(512)(128)(4,1)} %get-tuple-element.37) | copy-start | bytes 388
  1623.9 35.1 %all-to-all-start.11 = ((bf16[512,3,512]{2,1,0:T(4,128)(2,1)}), bf16[512,3,512]{2,1,0:T(4,128)(2,1)S(1)}, u32[]{:S(2)}, u32[]{:S(2)}) async-start(bf16[512,3,512]{2,1,0:T(4,128)(2,1)} %gather_fusion.26), calls=%async_computation.11 | async-start | bytes 4194304 | tf_op jit(solution)/shard_map/all_to_all | solution.py:170
  1660.1 1.2 copy-start.1
where the time goes:
time: 1680 us; the launch traced here: 1670 us
  local copies, waits for them, and re-layouts  1340 us (80%)
  waiting for transfers between devices  129 us (8%)
  starting transfers between devices  67.9 us (4%)
  blocking collectives  63 us (4%)
  other arithmetic  38.4 us (2%)
  matrix products  25.6 us (2%)
    gather x18, local copies, waits for them, and re-layouts, resolve_ghosts(): refined = jnp.take_along_axis(layers, table[quadrant], axis=1)  1260 us
    all_to_all x8, waiting for transfers between devices, faces_to_asker(): lax.all_to_all(wide.astype(jnp.bfloat16), 'hilbert', split_axis=0, concat...  81 us
    psum x1, blocking collectives, on_device(): mass_sum = lax.psum(jnp.sum(density), 'hilbert')  63 us
    all_to_all x8, starting transfers between devices, faces_to_asker(): lax.all_to_all(wide.astype(jnp.bfloat16), 'hilbert', split_axis=0, concat...  36.7 us
  transfers between devices with their start and end apart: 12, of which 11 were waited for; matrix products, arithmetic and copies ran while one was open for 2% of the time, Pallas kernels for 0%

commit v1 on v0

v1 whole, which is shorter than its diff:
```python
import jax
import jax.numpy as jnp
import numpy as np
from jax import lax
from jax.experimental import pallas as pl
from jax.experimental.pallas import tpu as pltpu
from jax.sharding import PartitionSpec as P

N = 128
B = 128
O = 64
C = 512
S = 64
F6 = 6 * S
PART = 256
OFFS = (1, 2, 3, 4, 127, 126, 125, 124, 64)
BACK = (4, 5, 6, 7, 0, 1, 2, 3, 8)
LANES = len(OFFS)
ROWS = 16 * LANES
TOTAL_CELLS = float(N * O * C)
COUPLING = 0.25
UNROLL = 8

f32 = jnp.float32
bf16 = jnp.bfloat16
i32 = jnp.int32


def dot(a, b):
    return jnp.dot(a, b, preferred_element_type=f32)


def dot_t(a, b):
    return lax.dot_general(a, b, (((0,), (0,)), ((), ())), preferred_element_type=f32)


def iota(shape, dim):
    return lax.broadcasted_iota(i32, shape, dim)


def static_tables():
    cell = np.arange(C)
    coords = (cell // 64, cell // 8 % 8, cell % 8)
    others = ((1, 2), (1, 2), (0, 2), (0, 2), (0, 1), (0, 1))
    pick = np.zeros((C, F6), np.float32)
    place = np.zeros((3, 256, C), np.float32)
    j = np.arange(S)
    ju, jv = j // 8, j % 8
    for f in range(6):
        own = 0 if f % 2 == 0 else 7
        x = coords[f // 2]
        u, v = coords[others[f][0]], coords[others[f][1]]
        spot = u * 8 + v
        pick[:, f * S : (f + 1) * S] = (x == 7 - own)[:, None] & (spot[:, None] == j[None, :])
        rows = slice((f % 2) * S, (f % 2 + 1) * S)
        on = (x == own)[None, :]
        place[f // 2, rows] = on & (spot[None, :] == j[:, None])
        rows = slice(128 + (f % 2) * S, 128 + (f % 2 + 1) * S)
        place[f // 2, rows] = (
            on & (u[None, :] // 2 == ju[:, None] % 4) & (v[None, :] // 2 == jv[:, None] % 4)
        )
    group = np.arange(F6) // S
    diag = (group[:, None] == group[None, :]).astype(np.float32)
    return pick, place.reshape(768, C), diag


def weights(row):
    centres = iota((8, PART), 0).astype(f32) + 0.5
    return jnp.maximum(0.0, 1.0 - jnp.abs(row - centres))


def crossed(wy, wz):
    full = jnp.concatenate([wy[y : y + 1] * wz for y in range(8)], axis=0)
    high = full.astype(bf16)
    return high, (full - high.astype(f32)).astype(bf16)


def kernel(
    pos_ref, mass_ref, block_ref, face_ref, pick_ref, place_ref, diag_ref,
    phi_ref, accel_ref,
    dep_ref, req_send, req_got, msg_send, dep_got, field_got, face_send, face_got,
    sum_send, sum_got, field_ref, dens_ref, m0_ref, mc_ref, home_ref, fmask_ref, smask_ref, gro_ref, os_ref,
    req_ss, req_rs, msg_ss, dep_rs, field_rs, face_ss, face_rs, sum_ss, sum_rs,
):
    me = lax.axis_index("hilbert")
    peers = [lax.rem(me + o, N) for o in OFFS]
    stages = []
    for stride, size in ((1, 2), (2, 4), (8, 4), (32, 4)):
        digit = lax.rem(me // stride, size)
        stages.append(
            [(me + (lax.rem(digit + j, size) - digit) * stride, size - 1 - j) for j in range(1, size)]
        )

    barrier = pltpu.get_barrier_semaphore()
    partners = peers + [p for stage in stages for p, _ in stage]
    for p in partners:
        pl.semaphore_signal(barrier, inc=1, device_id=(p,), device_id_type=pl.DeviceIdType.MESH)

    def send(src, dst, ss, rs, p):
        return pltpu.make_async_remote_copy(
            src_ref=src, dst_ref=dst, send_sem=ss, recv_sem=rs,
            device_id=(p,), device_id_type=pl.DeviceIdType.MESH,
        )

    lane128 = iota((1, 128), 1)
    offs_row = jnp.where(
        lane128 < 4,
        lane128 + 1,
        jnp.where(lane128 < 8, 131 - lane128, jnp.where(lane128 == 8, 64, -1)),
    )
    lane_f = lane128.astype(f32)

    def slots_of(match):
        rows = match.shape[0]
        earlier = (iota((rows, rows), 0) > iota((rows, rows), 1)).astype(f32).astype(bf16)
        rank = jnp.sum(dot(earlier, match.astype(bf16)) * match, axis=1, keepdims=True)
        lane = jnp.sum(match * lane_f, axis=1, keepdims=True)
        away = jnp.sum(match, axis=1, keepdims=True)
        return jnp.where(away > 0.5, lane * 16.0 + rank, -1000.0)

    face_cols = face_ref[...]
    group = iota((O, F6), 1) // S

    def spread(base):
        total = jnp.zeros((O, F6), i32)
        for f in range(6):
            total = jnp.where(group == f, face_cols[:, base + f : base + f + 1], total)
        return total

    inside = iota((O, F6), 1) % S
    delta = (face_cols[:, 0:6] - me + N) % N
    match = jnp.concatenate(
        [(delta[:, f : f + 1] == offs_row).astype(f32) for f in range(6)], axis=0
    )
    face_slot = slots_of(match)
    slot_row = iota((F6, ROWS), 1).astype(f32)
    takes = (face_slot == slot_row).astype(f32)
    gro = takes[0:O]
    for f in range(1, 6):
        gro = gro + takes[f * O : (f + 1) * O]
    gro_ref[...] = gro.astype(bf16)
    oct_col = jnp.concatenate([face_cols[:, 6 + f : 7 + f] for f in range(6)], axis=0)
    wide_lane = iota((F6, 512), 1)
    row_face = iota((F6, 512), 0) // O
    wanted = jnp.where(
        wide_lane < S,
        (oct_col == wide_lane).astype(f32),
        jnp.where(
            wide_lane < 128,
            (wide_lane - S == row_face).astype(f32),
            ((wide_lane - 128) // S == row_face).astype(f32),
        ),
    ).astype(bf16)
    asked = dot_t(takes.astype(bf16), wanted)
    smask_ref[...] = asked[:, 128:].astype(bf16)

    own_x = spread(0)
    home_ref[...] = ((own_x == me) & (spread(6) == inside)).astype(f32).astype(bf16)
    coarse_x = spread(12)
    quad_x = spread(18)
    quad_in = (inside // 32) * 2 + (inside % 8) // 4
    m0 = (coarse_x != 1).astype(f32).astype(bf16)
    mc = ((coarse_x == 1) & (quad_x == quad_in)).astype(f32).astype(bf16)
    m0_ref[...] = jnp.concatenate([m0, m0], axis=0)
    mc_ref[...] = jnp.concatenate([mc, mc], axis=0)

    block_cols = block_ref[...]
    block_delta = (block_cols[:, 0:1] - me + N) % N
    block_slot = slots_of((block_delta == offs_row).astype(f32))
    slot_lane = iota((B, ROWS), 1).astype(f32)
    into = [(block_slot + 4.0 * d == slot_lane).astype(f32).astype(bf16) for d in range(3)]
    oct_is = block_cols[:, 1:2] == iota((B, 128), 1)
    at_home = ((block_delta == 0) & oct_is).astype(f32).astype(bf16)
    oct_hot = oct_is.astype(f32).astype(bf16)
    block_oct_rows = dot_t(into[0] + into[1] + into[2], oct_hot)
    req_send[:, 0:128] = asked[:, 0:128].astype(bf16)
    req_send[:, 128:256] = block_oct_rows.astype(bf16)

    masses = mass_ref[...]
    tile = masses[0:8, 0:128]
    for r in range(16):
        for h in range(2):
            if r or h:
                tile = tile + masses[8 * r : 8 * r + 8, 128 * h : 128 * h + 128]

    pl.semaphore_wait(barrier, len(partners))

    requests = []
    for l in range(LANES):
        requests.append(
            send(
                req_send.at[pl.ds(16 * l, 16)], req_got.at[pl.ds(16 * BACK[l], 16)],
                req_ss.at[l], req_rs.at[BACK[l]], peers[l],
            )
        )
        requests[-1].start()

    def deposit(i, carry):
        for r in range(UNROLL):
            b = i * UNROLL + r
            p = pos_ref[b]
            wx = weights(p[0:1]) * mass_ref[pl.ds(b, 1), :]
            high, low = crossed(weights(p[1:2]), weights(p[2:3]))
            x_high = wx.astype(bf16).astype(f32)
            left = jnp.concatenate([x_high, wx - x_high], axis=0).astype(bf16)
            right = jnp.concatenate([high, low], axis=0)
            both = lax.dot_general(
                left, right, (((1,), (1,)), ((), ())), preferred_element_type=f32
            )
            dep_ref[pl.ds(pl.multiple_of(b * 8, 8), 8), :] = both[0:8] + both[8:16]
        return carry

    per = B // UNROLL // len(stages)
    sums = []
    n_sum = 0
    for s, stage in enumerate(stages):
        sum_send[s] = tile
        here = []
        for j, (p, back) in enumerate(stage):
            here.append(
                send(sum_send.at[s], sum_got.at[n_sum + back], sum_ss.at[n_sum + j], sum_rs.at[n_sum + back], p)
            )
            here[-1].start()
        lax.fori_loop(s * per, (s + 1) * per, deposit, 0)
        for copy in here:
            copy.wait_recv()
        for j in range(len(stage)):
            tile = tile + sum_got[n_sum + j]
        sums += here
        n_sum += len(stage)
    mean = jnp.sum(jnp.sum(tile, axis=0, keepdims=True), axis=1, keepdims=True) / TOTAL_CELLS

    low_half = iota((B, 128), 1) < S
    parts = []
    for i in range(4):
        even = dep_ref[pl.ds(2 * i, B, stride=8), :]
        odd = dep_ref[pl.ds(2 * i + 1, B, stride=8), :]
        parts.append(
            jnp.where(low_half, even + pltpu.roll(even, S, 1), odd + pltpu.roll(odd, S, 1))
        )
    rest = jnp.concatenate(parts, axis=1)
    pieces = []
    for _ in range(3):
        piece = rest.astype(bf16)
        rest = rest - piece.astype(f32)
        pieces.append(piece)
    stacked = jnp.concatenate(pieces, axis=0)
    msg_send[...] = dot_t(jnp.concatenate(into, axis=0), stacked).astype(bf16)
    deposits = []
    for l in range(LANES):
        deposits.append(
            send(
                msg_send.at[pl.ds(16 * l, 16)], dep_got.at[pl.ds(16 * BACK[l], 16)],
                msg_ss.at[l], dep_rs.at[BACK[l]], peers[l],
            )
        )
        deposits[-1].start()
    density = dot_t(jnp.concatenate([at_home] * 3, axis=0), stacked)[0:O]

    for copy in requests:
        copy.wait_recv()
    asks = req_got[...]
    os_ref[...] = asks[:, 0:S]
    to_face = (iota((128, F6), 0) - S == iota((128, F6), 1) // S).astype(f32).astype(bf16)
    fmask_ref[...] = dot(asks[:, 0:128], to_face)
    slot_octs = asks[:, 128 : 128 + S]

    for copy in deposits:
        copy.wait_recv()
    density = density + dot_t(slot_octs, dep_got[...])
    source = COUPLING * (density - mean)
    dens_ref[...] = source
    phi_ref[...] = source * (-1.0 / 6.0)

    lane = iota((1, C), 1)
    at = (lane // 64, lane // 8 % 8, lane % 8)
    strides = (64, 8, 1)

    def inner(phi, d):
        up = jnp.where(at[d] < 7, pltpu.roll(phi, C - strides[d], 1), 0.0)
        down = jnp.where(at[d] > 0, pltpu.roll(phi, strides[d], 1), 0.0)
        return up, down

    def placed(raw, d, sign):
        rows = raw.shape[0]
        part = raw[:, 128 * d : 128 * d + 128]
        if sign is not None:
            part = part * sign
        left = jnp.concatenate(
            [part * m0_ref[0:rows, 128 * d : 128 * d + 128], part * mc_ref[0:rows, 128 * d : 128 * d + 128]],
            axis=1,
        )
        return dot(left, place_ref[256 * d : 256 * d + 256, :])

    def exchange_start(phi, slot):
        high = phi.astype(bf16)
        layers = dot(high, pick_ref[...]).astype(bf16)
        chosen = dot(os_ref[...], layers) * fmask_ref[...]
        out = chosen[:, 0:128] + chosen[:, 128:256] + chosen[:, 256:384]
        face_send[...] = (out + pltpu.roll(out, S, 1)).astype(bf16)
        copies = []
        for l in range(LANES):
            copies.append(
                send(
                    face_send.at[pl.ds(16 * l, 16)], face_got.at[slot, pl.ds(16 * BACK[l], 16)],
                    face_ss.at[l], face_rs.at[slot, BACK[l]], peers[l],
                )
            )
            copies[-1].start()
        return high, layers, copies

    def home_ghosts(phi, high, layers):
        low = (phi - high.astype(f32)).astype(bf16)
        layers_low = dot(low, pick_ref[...]).astype(bf16)
        diag = diag_ref[...]
        wide = [jnp.concatenate([x] * 6, axis=0) * diag for x in (layers, layers_low)]
        return jnp.concatenate([dot(home_ref[...], x).astype(bf16) for x in wide], axis=0)

    def away_ghosts(slot):
        got = face_got[slot]
        return dot(gro_ref[...], jnp.concatenate([got] * 3, axis=1) * smask_ref[...]).astype(bf16)

    def sweep(k, carry):
        slot = lax.rem(k, 2)
        phi = phi_ref[...]
        high, layers, copies = exchange_start(phi, slot)
        raw = home_ghosts(phi, high, layers)
        total = placed(raw, 0, None) + placed(raw, 1, None) + placed(raw, 2, None)
        total = total[0:O] + total[O : 2 * O] - dens_ref[...]
        for d in range(3):
            up, down = inner(phi, d)
            total = total + (up + down)
        for copy in copies:
            copy.wait_recv()
        raw = away_ghosts(slot)
        total = total + (placed(raw, 0, None) + placed(raw, 1, None) + placed(raw, 2, None))
        phi_ref[...] = total * (1.0 / 6.0)
        for copy in copies:
            copy.wait_send()
        return carry

    lax.fori_loop(1, 8, sweep, 0)

    for copy in deposits:
        copy.wait_send()
    phi = phi_ref[...]
    high, layers, copies = exchange_start(phi, 0)
    sign = jnp.where(iota((1, 128), 1) < S, 0.5, -0.5).astype(bf16)
    raw = home_ghosts(phi, high, layers)
    near = []
    for d in range(3):
        up, down = inner(phi, d)
        part = placed(raw, d, sign)
        near.append(0.5 * (down - up) + part[0:O] + part[O : 2 * O])
    for copy in copies:
        copy.wait_recv()
    raw = away_ghosts(0)
    field = [(near[d] + placed(raw, d, sign)).astype(bf16) for d in range(3)]
    row_dim = iota((ROWS, 1), 0) % 16 // 4
    picked = [dot(slot_octs, field[d]) for d in range(3)]
    msg_send[...] = jnp.where(
        row_dim == 0, picked[0], jnp.where(row_dim == 1, picked[1], picked[2])
    ).astype(bf16)
    returns = []
    for l in range(LANES):
        returns.append(
            send(
                msg_send.at[pl.ds(16 * l, 16)], field_got.at[pl.ds(16 * BACK[l], 16)],
                msg_ss.at[l], field_rs.at[BACK[l]], peers[l],
            )
        )
        returns[-1].start()
    mine = [dot(at_home[:, 0:O], field[d]) for d in range(3)]
    for copy in returns:
        copy.wait_recv()
    got = field_got[...]
    for d in range(3):
        values = mine[d] + dot(into[d], got)
        for i in range(4):
            pair = values[:, 128 * i : 128 * i + 128]
            turned = pltpu.roll(pair, S, 1)
            field_ref[d, pl.ds(2 * i, B, stride=8), :] = jnp.where(low_half, pair, turned)
            field_ref[d, pl.ds(2 * i + 1, B, stride=8), :] = jnp.where(low_half, turned, pair)

    def interpolate(i, carry):
        for r in range(UNROLL):
            b = i * UNROLL + r
            p = pos_ref[b]
            wx = weights(p[0:1])
            high, low = crossed(weights(p[1:2]), weights(p[2:3]))
            rows = pl.ds(pl.multiple_of(b * 8, 8), 8)
            left = jnp.concatenate([field_ref[d, rows, :] for d in range(3)], axis=0).astype(bf16)
            value = dot(left, jnp.concatenate([high, low], axis=0))
            accel_ref[b] = jnp.concatenate(
                [jnp.sum(value[8 * d : 8 * d + 8] * wx, axis=0, keepdims=True) for d in range(3)],
                axis=0,
            )
        return carry

    lax.fori_loop(0, B // UNROLL, interpolate, 0)

    for copy in requests + sums + copies + returns:
        copy.wait_send()


def on_device(
    positions, masses, block_owner, block_oct, face_owner, face_oct, face_coarse, face_quadrant
):
    blocks = jnp.concatenate([block_owner, block_oct[:, None]], axis=1)
    faces = jnp.concatenate([face_owner[:, :, 0], face_oct, face_coarse, face_quadrant], axis=1)
    pick, place, diag = static_tables()
    dma = pltpu.SemaphoreType.DMA
    vmem = pl.BlockSpec(memory_space=pltpu.VMEM)
    return pl.pallas_call(
        kernel,
        out_shape=(
            jax.ShapeDtypeStruct((O, C), f32),
            jax.ShapeDtypeStruct((B, 3, PART), f32),
        ),
        in_specs=[vmem] * 7,
        out_specs=(vmem, vmem),
        scratch_shapes=[
            pltpu.VMEM((B * 8, 128), f32),
            pltpu.VMEM((ROWS, 256), bf16),
            pltpu.VMEM((ROWS, 256), bf16),
            pltpu.VMEM((ROWS, C), bf16),
            pltpu.VMEM((ROWS, C), bf16),
            pltpu.VMEM((ROWS, C), bf16),
            pltpu.VMEM((ROWS, 128), bf16),
            pltpu.VMEM((2, ROWS, 128), bf16),
            pltpu.VMEM((4, 8, 128), f32),
            pltpu.VMEM((10, 8, 128), f32),
            pltpu.VMEM((3, B * 8, 128), f32),
            pltpu.VMEM((O, C), f32),
            pltpu.VMEM((2 * O, F6), bf16),
            pltpu.VMEM((2 * O, F6), bf16),
            pltpu.VMEM((O, F6), bf16),
            pltpu.VMEM((ROWS, F6), f32),
            pltpu.VMEM((ROWS, F6), bf16),
            pltpu.VMEM((O, ROWS), bf16),
            pltpu.VMEM((ROWS, S), bf16),
            dma((LANES,)),
            dma((LANES,)),
            dma((LANES,)),
            dma((LANES,)),
            dma((LANES,)),
            dma((LANES,)),
            dma((2, LANES)),
            dma((10,)),
            dma((10,)),
        ],
        compiler_params=pltpu.CompilerParams(
            collective_id=0, has_side_effects=True, vmem_limit_bytes=40 * 1024 * 1024
        ),
    )(
        positions,
        masses,
        blocks,
        faces,
        jnp.asarray(pick, bf16),
        jnp.asarray(place, bf16),
        jnp.asarray(diag, bf16),
    )


def solution(mesh):
    placed = (
        P("hilbert", None, None),
        P("hilbert", None),
        P("hilbert", None),
        P("hilbert"),
        P("hilbert", None, None),
        P("hilbert", None),
        P("hilbert", None),
        P("hilbert", None),
    )
    return jax.shard_map(
        on_device,
        mesh=mesh,
        in_specs=placed,
        out_specs=(P("hilbert", None), P("hilbert", None, None)),
        check_vma=False,
    )
```

time: 1680 us -> 96.5 us (0.06)
  local copies, waits for them, and re-layouts: 1340 us -> 5.62 us
  waiting for transfers between devices: 129 us -> 0 us
  Pallas kernels: 0 us -> 88.4 us
  starting transfers between devices: 67.9 us -> 0 us
  blocking collectives: 63 us -> 0 us
  other arithmetic: 38.4 us -> 1.48 us
  matrix products: 25.6 us -> 0 us
    gather x47 -> x0, local copies, waits for them, and re-layouts: 1310 us -> none  [the longest x18 1260 us: resolve_ghosts(): refined = jnp.take_along_axis(layers, table[quadrant], axis=1)]
    all_to_all x12 -> x0, waiting for transfers between devices: 129 us -> none  [the longest x8 81 us: faces_to_asker(): lax.all_to_all(wide.astype(jnp.bfloat16), 'hilbert', split_axis=0, concat...]
    pallas_call x0 -> x1, Pallas kernels: none -> 88.4 us  [on_device(): pl.pallas_call(kernel, out_shape=(jax.ShapeDtypeStruct((O, C), f32), jax....]
    all_to_all x12 -> x0, starting transfers between devices: 67.9 us -> none  [the longest x8 36.7 us: faces_to_asker(): lax.all_to_all(wide.astype(jnp.bfloat16), 'hilbert', split_axis=0, concat...]
    psum x1 -> x0, blocking collectives: 63 us -> none  [on_device(): mass_sum = lax.psum(jnp.sum(density), 'hilbert')]
    dot_general x25 -> x0, matrix products: 25.6 us -> none  [the longest x1 9.14 us: deposit_block(): jnp.einsum('mle,mbe->mlb', weighted_x, crossed_faces, precision=highest_l...]
    convert_element_type x17 -> x0, other arithmetic: 23 us -> none  [the longest x8 14.2 us: faces_to_asker(): wide.astype(jnp.bfloat16)]
  transfers between devices with their start and end apart: 12 -> 0, of which waited for: 11 -> 0; matrix products, arithmetic and copies ran while one was open for 2% -> 0% of each run, Pallas kernels for 0% -> 0%
where the time goes in v1:
time: 96.5 us; the launch traced here: 96.2 us
  Pallas kernels  88.4 us (92%)
  local copies, waits for them, and re-layouts  5.62 us (6%)
  other arithmetic  1.48 us (2%)
    pallas_call x1, Pallas kernels, on_device(): pl.pallas_call(kernel, out_shape=(jax.ShapeDtypeStruct((O, C), f32), jax....  88.4 us
    unnamed x11, local copies, waits for them, and re-layouts  4.61 us

profile of v1, /device:TPU:1, one launch (start us, length us, event | category | flops | bytes accessed | tf_op | source)
XLA Modules:
  0.0 96.2 jit_solution(17352649405756046973)
XLA Ops:
  0.6 0.0 copy-start
  0.6 0.8 pad_add_fusion.1
  1.4 0.7 copy.27
  2.1 0.7 pad_add_fusion
  2.8 0.1 copy.23.face_ref
  2.9 0.1 copy.22.block_ref
  3.0 0.0 copy-start.3
  3.0 1.3 %copy.21.pos_ref = f32[128,3,256]{2,1,0:T(4,128)S(1)} copy(f32[128,3,256]{2,0,1:T(8,128)} %param.11) | data formatting | bytes 786432 | tf_op args[0]
  4.3 0.0 copy-done
  4.3 0.0 copy-done.3
  4.3 0.0 copy-start.1
  4.4 1.0 %copy-done.1 = bf16[512,384]{1,0:T(8,128)(2,1)S(1)} copy-done((bf16[512,384]{1,0:T(8,128)(2,1)S(1)}, bf16[512,384]{1,0:T(8,128)(2,1)}, u32[]{:S(2)}) %copy-start.1) | copy-done | bytes 393240
  5.3 0.0 copy-start.2
  5.3 1.0 copy-done.2
  6.3 88.4 %shard_map.122 = (f32[64,512]{1,0:T(8,128)S(1)}, f32[128,3,256]{2,1,0:T(4,128)S(1)}) custom-call(f32[128,3,256]{2,1,0:T(4,128)S(1)} %copy.21.pos_ref, f32[128,256]{1,0:T(8,128)S(1)} %copy-done.3, s32[128,2]{1,0:T(8,128)S(1)} %copy.22.block_ref, s32[64,24]{1,0:T(8,128)S(1)} %copy.23.face_ref, bf16[512,384]{1,0:T(8,128)(2,1)S(1)} %copy-done.1, ...), custom_call_target="tpu_custom_call" | custom-call | tf_op jit(solution)/shard_map/pallas_call | solution.py:414
  94.7 0.8 copy.24
  95.5 0.7 copy.29
Async XLA Ops:
  0.6 3.7 %copy-start = (bf16[768,512]{1,0:T(8,128)(2,1)S(1)}, bf16[768,512]{1,0:T(8,128)(2,1)}, u32[]{:S(2)}) copy-start(bf16[768,512]{1,0:T(8,128)(2,1)} %constant.7.clone.place_ref) | copy-start | bytes 2359300
  3.0 1.3 %copy-start.3 = (f32[128,256]{1,0:T(8,128)S(1)}, f32[128,256]{1,0:T(8,128)}, u32[]{:S(2)}) copy-start(f32[128,256]{1,0:T(8,128)} %mass_ref.1) | copy-start | bytes 393220
  4.3 1.0 %copy-start.1 = (bf16[512,384]{1,0:T(8,128)(2,1)S(1)}, bf16[512,384]{1,0:T(8,128)(2,1)}, u32[]{:S(2)}) copy-start(bf16[512,384]{1,0:T(8,128)(2,1)} %constant.6.clone.pick_ref) | copy-start | bytes 1179652
  5.3 1.0 copy-start.2

commit v2 on v1

v2 whole, which is shorter than its diff:
```python
import jax
import jax.numpy as jnp
from jax import lax
from jax.experimental import pallas as pl
from jax.experimental.pallas import tpu as pltpu
from jax.sharding import PartitionSpec as P

N = 128
B = 128
O = 64
C = 512
S = 64
F6 = 6 * S
PART = 256
OFFS = (1, 2, 3, 4, 127, 126, 125, 124, 64)
BACK = (4, 5, 6, 7, 0, 1, 2, 3, 8)
LANES = len(OFFS)
LANE_ORDER = (8, 3, 7, 2, 6, 1, 5, 0, 4)
ROWS = 16 * LANES
TOTAL_CELLS = float(N * O * C)
COUPLING = 0.25

f32 = jnp.float32
bf16 = jnp.bfloat16
i32 = jnp.int32


def dot(a, b):
    return jnp.dot(a, b, preferred_element_type=f32)


def dot_t(a, b):
    return lax.dot_general(a, b, (((0,), (0,)), ((), ())), preferred_element_type=f32)


def iota(shape, dim):
    return lax.broadcasted_iota(i32, shape, dim)


def pick_table(d):
    cell, lane = iota((C, 128), 0), iota((C, 128), 1)
    coord, spot = cell_spot(cell, d)
    return ((coord == jnp.where(lane < S, 7, 0)) & (spot == lane % S)).astype(f32).astype(bf16)


def place_table(d):
    row, cell = iota((256, C), 0), iota((256, C), 1)
    coord, spot = cell_spot(cell, d)
    j = row % S
    here = coord == (row // S % 2) * 7
    fine = spot == j
    coarse = ((spot // 16) == (j // 8 % 4)) & ((spot % 8) // 2 == j % 4)
    return (here & (((row < 128) & fine) | ((row >= 128) & coarse))).astype(f32).astype(bf16)


def cell_spot(cell, d):
    x, y, z = cell // 64, cell // 8 % 8, cell % 8
    return ((x, y * 8 + z), (y, x * 8 + z), (z, x * 8 + y))[d]


def weights(row):
    centres = iota((8, PART), 0).astype(f32) + 0.5
    return jnp.maximum(0.0, 1.0 - jnp.abs(row - centres))


def crossed(wy, wz):
    full = jnp.concatenate([wy[y : y + 1] * wz for y in range(8)], axis=0)
    high = full.astype(bf16)
    return high, (full - high.astype(f32)).astype(bf16)


def device_at(x, z, y, core):
    return x * 32 + z * 8 + y * 2 + core


def host_of(i):
    x, z, y = i // 32, lax.rem(i // 8, 4), lax.rem(i // 2, 4)
    return device_at(
        lax.rem(x + 3, 4),
        z + lax.rem(x, 2) * (3 - 2 * z),
        y + lax.rem(z, 2) * (3 - 2 * y),
        lax.rem(i, 2),
    )


def hosted_by(i):
    x, z, y = lax.rem(i // 32 + 1, 4), lax.rem(i // 8, 4), lax.rem(i // 2, 4)
    z = z + lax.rem(x, 2) * (3 - 2 * z)
    return device_at(x, z, y + lax.rem(z, 2) * (3 - 2 * y), lax.rem(i, 2))


def kernel(
    pos_ref, mass_ref, bown_ref, boct_ref, fown_ref, foct_ref, fco_ref, fq_ref,
    phi_ref, accel_ref,
    dep_ref, req_send, req_got, msg_send, dep_got, field_got, face_send, face_got,
    sum_send, sum_got, field_ref, dens_ref, m0_ref, mc_ref, home_ref, fmask_ref, smask_ref, gro_ref, os_ref,
    pick_ref, place_ref, diag_ref, index_ref, index_got, home_send, home_got, fhome_send, fhome_got,
    work_ref, phi_got,
    req_ss, req_rs, msg_ss, dep_rs, field_rs, face_ss, face_rs, sum_ss, sum_rs, one_ss, one_rs,
):
    me = lax.axis_index("hilbert")
    owner = hosted_by(me)
    my_host = host_of(me)
    near = [lax.rem(me + o, N) for o in OFFS]
    hosts = [host_of(p) for p in near]
    holders = [lax.rem(owner + o, N) for o in OFFS]
    peers = [host_of(p) for p in holders]
    stages = []
    for stride, size in ((1, 2), (2, 4), (8, 4), (32, 4)):
        digit = lax.rem(me // stride, size)
        stages.append(
            [(me + (lax.rem(digit + j, size) - digit) * stride, size - 1 - j) for j in range(1, size)]
        )
    first_sum = (0, 1, 4, 7)

    barrier = pltpu.get_barrier_semaphore()
    partners = peers + hosts + holders + [my_host, owner] + [p for stage in stages for p, _ in stage]
    for p in partners:
        pl.semaphore_signal(barrier, inc=1, device_id=(p,), device_id_type=pl.DeviceIdType.MESH)

    def send(src, dst, ss, rs, p):
        copy = pltpu.make_async_remote_copy(
            src_ref=src, dst_ref=dst, send_sem=ss, recv_sem=rs,
            device_id=(p,), device_id_type=pl.DeviceIdType.MESH,
        )
        copy.start()
        return copy

    def send_lanes(src, dst, ss, rs, to):
        return [
            send(
                src.at[pl.ds(16 * l, 16)], dst.at[pl.ds(16 * BACK[l], 16)],
                ss.at[l], rs.at[BACK[l]], to[l],
            )
            for l in LANE_ORDER
        ]

    lane128 = iota((1, 128), 1)
    offs_row = jnp.where(
        lane128 < 4,
        lane128 + 1,
        jnp.where(lane128 < 8, 131 - lane128, jnp.where(lane128 == 8, 64, -1)),
    )
    lane_f = lane128.astype(f32)

    def slots_of(match):
        rows = match.shape[0]
        earlier = (iota((rows, rows), 0) > iota((rows, rows), 1)).astype(f32).astype(bf16)
        rank = jnp.sum(dot(earlier, match.astype(bf16)) * match, axis=1, keepdims=True)
        lane = jnp.sum(match * lane_f, axis=1, keepdims=True)
        away = jnp.sum(match, axis=1, keepdims=True)
        return jnp.where(away > 0.5, lane * 16.0 + rank, -1000.0)

    def face_slots(columns, of):
        delta = (columns[0:O, 0:6] - of + N) % N
        match = jnp.concatenate(
            [(delta[:, f : f + 1] == offs_row).astype(f32) for f in range(6)], axis=0
        )
        return (slots_of(match) == iota((F6, ROWS), 1).astype(f32)).astype(f32)

    index_ref[...] = jnp.zeros((128, 128), f32)
    for f in range(6):
        index_ref[f : f + 1, 0:O] = fown_ref[f].astype(f32)
        index_ref[8 + f : 9 + f, 0:O] = foct_ref[f : f + 1].astype(f32)
        index_ref[16 + f : 17 + f, 0:O] = fco_ref[f : f + 1].astype(f32)
        index_ref[24 + f : 25 + f, 0:O] = fq_ref[f : f + 1].astype(f32)
    index_ref[32:33, :] = bown_ref[...].astype(f32)
    index_ref[33:34, :] = boct_ref[...].astype(f32)
    columns = index_ref[...].T.astype(i32)

    takes = face_slots(columns, me)
    oct_col = jnp.concatenate([columns[0:O, 8 + f : 9 + f] for f in range(6)], axis=0)
    lane_wide = iota((F6, 128), 1)
    row_face = iota((F6, 128), 0) // O
    wanted = jnp.where(
        lane_wide < S, (oct_col == lane_wide).astype(f32), (lane_wide - S == row_face).astype(f32)
    ).astype(bf16)

    block_delta = (columns[:, 32:33] - me + N) % N
    block_slot = slots_of((block_delta == offs_row).astype(f32))
    slot_lane = iota((B, ROWS), 1).astype(f32)
    into = [(block_slot + 4.0 * d == slot_lane).astype(f32).astype(bf16) for d in range(3)]
    oct_is = columns[:, 33:34] == iota((B, 128), 1)
    at_home = ((block_delta == 0) & oct_is).astype(f32).astype(bf16)
    oct_hot = oct_is.astype(f32).astype(bf16)
    req_send[:, 0:128] = dot_t(takes.astype(bf16), wanted).astype(bf16)
    req_send[:, 128:256] = dot_t(into[0] + into[1] + into[2], oct_hot).astype(bf16)

    masses = mass_ref[...]
    tile = masses[0:8, 0:128]
    for r in range(16):
        for h in range(2):
            if r or h:
                tile = tile + masses[8 * r : 8 * r + 8, 128 * h : 128 * h + 128]

    def deposit(i, carry):
        rows = pl.ds(pl.multiple_of(i * 8, 8), 8)
        xs, ys, zs, ms = pos_ref[0, rows, :], pos_ref[1, rows, :], pos_ref[2, rows, :], mass_ref[rows, :]
        for r in range(8):
            wx = weights(xs[r : r + 1]) * ms[r : r + 1]
            high, low = crossed(weights(ys[r : r + 1]), weights(zs[r : r + 1]))
            x_high = wx.astype(bf16).astype(f32)
            left = jnp.concatenate([x_high, wx - x_high], axis=0).astype(bf16)
            right = jnp.concatenate([high, low], axis=0)
            both = lax.dot_general(
                left, right, (((1,), (1,)), ((), ())), preferred_element_type=f32
            )
            dep_ref[pl.ds(pl.multiple_of(i * 64 + 8 * r, 8), 8), :] = both[0:8] + both[8:16]
        return carry

    lax.fori_loop(0, B // 8, deposit, 0)

    low_half = iota((B, 128), 1) < S
    parts = []
    for i in range(4):
        even = dep_ref[pl.ds(2 * i, B, stride=8), :]
        odd = dep_ref[pl.ds(2 * i + 1, B, stride=8), :]
        parts.append(
            jnp.where(low_half, even + pltpu.roll(even, S, 1), odd + pltpu.roll(odd, S, 1))
        )
    rest = jnp.concatenate(parts, axis=1)
    pieces = []
    for _ in range(3):
        piece = rest.astype(bf16)
        rest = rest - piece.astype(f32)
        pieces.append(piece)
    stacked = jnp.concatenate(pieces, axis=0)
    home_send[...] = dot_t(jnp.concatenate([at_home] * 3, axis=0), stacked)[0:O]
    msg_send[...] = dot_t(jnp.concatenate(into, axis=0), stacked).astype(bf16)

    pl.semaphore_wait(barrier, len(partners))

    index_copy = send(index_ref.at[pl.ds(0, 32)], index_got, one_ss.at[0], one_rs.at[0], my_host)
    home_copy = send(home_send, home_got, one_ss.at[1], one_rs.at[1], my_host)
    deposits = send_lanes(msg_send, dep_got, msg_ss, dep_rs, hosts)
    requests = send_lanes(req_send, req_got, req_ss, req_rs, hosts)
    sums = []

    def sum_start(s, tile):
        sum_send[s] = tile
        for j, (p, back) in enumerate(stages[s]):
            at = first_sum[s]
            sums.append(
                send(sum_send.at[s], sum_got.at[at + back], sum_ss.at[at + j], sum_rs.at[at + back], p)
            )

    def sum_end(s, tile):
        at, count = first_sum[s], len(stages[s])
        for copy in sums[at : at + count]:
            copy.wait_recv()
        for j in range(count):
            tile = tile + sum_got[at + j]
        return tile

    sum_start(0, tile)

    for d in range(3):
        pick_ref[:, 128 * d : 128 * d + 128] = pick_table(d)
        place_ref[256 * d : 256 * d + 256, :] = place_table(d)
    diag_ref[...] = (iota((F6, F6), 0) // S == iota((F6, F6), 1) // S).astype(f32).astype(bf16)
    to_face = (iota((128, F6), 0) - S == iota((128, F6), 1) // S).astype(f32).astype(bf16)

    tile = sum_end(0, tile)
    sum_start(1, tile)

    index_copy.wait_recv()
    spare = jnp.zeros((96, 128), f32)
    columns = jnp.concatenate([index_got[...], spare], axis=0).T.astype(i32)
    group = iota((O, F6), 1) // S

    def spread(base):
        total = jnp.zeros((O, F6), i32)
        for f in range(6):
            total = jnp.where(group == f, columns[0:O, base + f : base + f + 1], total)
        return total

    takes = face_slots(columns, owner)
    gro = takes[0:O]
    for f in range(1, 6):
        gro = gro + takes[f * O : (f + 1) * O]
    gro_ref[...] = gro.astype(bf16)
    same_face = (iota((F6, F6), 0) // O == iota((F6, F6), 1) // S).astype(f32).astype(bf16)
    smask_ref[...] = dot_t(takes.astype(bf16), same_face).astype(bf16)
    inside = iota((O, F6), 1) % S
    home_ref[...] = ((spread(0) == owner) & (spread(8) == inside)).astype(f32).astype(bf16)
    coarse_x = spread(16)
    quad_x = spread(24)
    quad_in = (inside // 32) * 2 + (inside % 8) // 4
    m0 = (coarse_x != 1).astype(f32).astype(bf16)
    mc = ((coarse_x == 1) & (quad_x == quad_in)).astype(f32).astype(bf16)
    m0_ref[...] = jnp.concatenate([m0, m0], axis=0)
    mc_ref[...] = jnp.concatenate([mc, mc], axis=0)

    for copy in requests:
        copy.wait_recv()
    asks = req_got[...]
    os_ref[...] = asks[:, 0:S]
    fmask_ref[...] = dot(asks[:, 0:128], to_face)
    slot_octs = asks[:, 128 : 128 + S]

    for copy in deposits:
        copy.wait_recv()
    density = dot_t(slot_octs, dep_got[...])
    home_copy.wait_recv()
    source = COUPLING * (density + home_got[...])
    dens_ref[...] = source
    work_ref[...] = source * (-1.0 / 6.0)

    lane = iota((1, C), 1)
    at = (lane // 64, lane // 8 % 8, lane % 8)
    strides = (64, 8, 1)

    def inner(phi, d):
        up = jnp.where(at[d] < 7, pltpu.roll(phi, C - strides[d], 1), 0.0)
        down = jnp.where(at[d] > 0, pltpu.roll(phi, strides[d], 1), 0.0)
        return up, down

    def placed(raw, d, sign):
        rows = raw.shape[0]
        part = raw[:, 128 * d : 128 * d + 128]
        if sign is not None:
            part = part * sign
        left = jnp.concatenate(
            [part * m0_ref[0:rows, 128 * d : 128 * d + 128], part * mc_ref[0:rows, 128 * d : 128 * d + 128]],
            axis=1,
        )
        return dot(left, place_ref[256 * d : 256 * d + 256, :])

    def exchange_start(phi, slot):
        high = phi.astype(bf16)
        layers = dot(high, pick_ref[...]).astype(bf16)
        chosen = dot(os_ref[...], layers) * fmask_ref[...]
        out = chosen[:, 0:128] + chosen[:, 128:256] + chosen[:, 256:384]
        face_send[...] = (out + pltpu.roll(out, S, 1)).astype(bf16)
        copies = send_lanes(face_send, face_got.at[slot], face_ss, face_rs.at[slot], peers)
        return high, layers, copies

    def home_ghosts(phi, high, layers):
        low = (phi - high.astype(f32)).astype(bf16)
        layers_low = dot(low, pick_ref[...]).astype(bf16)
        diag = diag_ref[...]
        wide = [jnp.concatenate([x] * 6, axis=0) * diag for x in (layers, layers_low)]
        return jnp.concatenate([dot(home_ref[...], x).astype(bf16) for x in wide], axis=0)

    def away_ghosts(slot):
        got = face_got[slot]
        return dot(gro_ref[...], jnp.concatenate([got] * 3, axis=1) * smask_ref[...]).astype(bf16)

    def sweep(slot, between):
        phi = work_ref[...]
        high, layers, copies = exchange_start(phi, slot)
        between()
        raw = home_ghosts(phi, high, layers)
        total = placed(raw, 0, None) + placed(raw, 1, None) + placed(raw, 2, None)
        total = total[0:O] + total[O : 2 * O] - dens_ref[...]
        for d in range(3):
            up, down = inner(phi, d)
            total = total + (up + down)
        for copy in copies:
            copy.wait_recv()
        raw = away_ghosts(slot)
        total = total + (placed(raw, 0, None) + placed(raw, 1, None) + placed(raw, 2, None))
        work_ref[...] = total * (1.0 / 6.0)
        for copy in copies:
            copy.wait_send()

    tiles = [tile]

    def step_sum(s):
        tiles.append(sum_end(s, tiles[-1]))
        if s < 3:
            sum_start(s + 1, tiles[-1])

    for k in range(1, 4):
        sweep(k % 2, lambda: step_sum(k))
    total = jnp.sum(jnp.sum(tiles[-1], axis=0, keepdims=True), axis=1, keepdims=True)
    mean = total * (COUPLING / TOTAL_CELLS)
    work_ref[...] = work_ref[...] + mean * (4.0 / 6.0)
    dens_ref[...] = dens_ref[...] - mean

    def later(k, carry):
        sweep(lax.rem(k, 2), lambda: None)
        return carry

    lax.fori_loop(4, 8, later, 0)

    for copy in deposits:
        copy.wait_send()
    phi = work_ref[...]
    high, layers, copies = exchange_start(phi, 0)
    phi_copy = send(work_ref, phi_got, one_ss.at[3], one_rs.at[3], owner)
    sign = jnp.where(iota((1, 128), 1) < S, 0.5, -0.5).astype(bf16)
    raw = home_ghosts(phi, high, layers)
    local = []
    for d in range(3):
        up, down = inner(phi, d)
        part = placed(raw, d, sign)
        local.append(0.5 * (down - up) + part[0:O] + part[O : 2 * O])
    for copy in copies:
        copy.wait_recv()
    raw = away_ghosts(0)
    field = [(local[d] + placed(raw, d, sign)).astype(bf16) for d in range(3)]
    fhome_send[...] = jnp.concatenate(field, axis=0)
    fhome_copy = send(fhome_send, fhome_got, one_ss.at[2], one_rs.at[2], owner)
    row_dim = iota((ROWS, 1), 0) % 16 // 4
    picked = [dot(slot_octs, field[d]) for d in range(3)]
    msg_send[...] = jnp.where(
        row_dim == 0, picked[0], jnp.where(row_dim == 1, picked[1], picked[2])
    ).astype(bf16)
    returns = send_lanes(msg_send, field_got, msg_ss, field_rs, holders)
    phi_copy.wait_recv()
    phi_ref[...] = phi_got[...]
    fhome_copy.wait_recv()
    for copy in returns:
        copy.wait_recv()
    got = field_got[...]
    for d in range(3):
        values = dot(at_home[:, 0:O], fhome_got[O * d : O * d + O]) + dot(into[d], got)
        for i in range(4):
            pair = values[:, 128 * i : 128 * i + 128]
            turned = pltpu.roll(pair, S, 1)
            field_ref[d, pl.ds(2 * i, B, stride=8), :] = jnp.where(low_half, pair, turned)
            field_ref[d, pl.ds(2 * i + 1, B, stride=8), :] = jnp.where(low_half, turned, pair)

    def interpolate(i, carry):
        rows = pl.ds(pl.multiple_of(i * 8, 8), 8)
        xs, ys, zs = pos_ref[0, rows, :], pos_ref[1, rows, :], pos_ref[2, rows, :]
        out = [[], [], []]
        for r in range(8):
            wx = weights(xs[r : r + 1])
            high, low = crossed(weights(ys[r : r + 1]), weights(zs[r : r + 1]))
            at = pl.ds(pl.multiple_of(i * 64 + 8 * r, 8), 8)
            left = jnp.concatenate([field_ref[d, at, :] for d in range(3)], axis=0).astype(bf16)
            value = dot(left, jnp.concatenate([high, low], axis=0))
            for d in range(3):
                out[d].append(jnp.sum(value[8 * d : 8 * d + 8] * wx, axis=0, keepdims=True))
        for d in range(3):
            accel_ref[d, rows, :] = jnp.concatenate(out[d], axis=0)
        return carry

    lax.fori_loop(0, B // 8, interpolate, 0)

    for copy in [index_copy, home_copy, phi_copy, fhome_copy] + requests + sums + copies + returns:
        copy.wait_send()


def on_device(
    positions, masses, block_owner, block_oct, face_owner, face_oct, face_coarse, face_quadrant
):
    dma = pltpu.SemaphoreType.DMA
    vmem = pl.BlockSpec(memory_space=pltpu.VMEM)
    potential, accel = pl.pallas_call(
        kernel,
        out_shape=(
            jax.ShapeDtypeStruct((O, C), f32),
            jax.ShapeDtypeStruct((3, B, PART), f32),
        ),
        in_specs=[vmem] * 8,
        out_specs=(vmem, vmem),
        scratch_shapes=[
            pltpu.VMEM((B * 8, 128), f32),
            pltpu.VMEM((ROWS, 256), bf16),
            pltpu.VMEM((ROWS, 256), bf16),
            pltpu.VMEM((ROWS, C), bf16),
            pltpu.VMEM((ROWS, C), bf16),
            pltpu.VMEM((ROWS, C), bf16),
            pltpu.VMEM((ROWS, 128), bf16),
            pltpu.VMEM((2, ROWS, 128), bf16),
            pltpu.VMEM((4, 8, 128), f32),
            pltpu.VMEM((10, 8, 128), f32),
            pltpu.VMEM((3, B * 8, 128), f32),
            pltpu.VMEM((O, C), f32),
            pltpu.VMEM((2 * O, F6), bf16),
            pltpu.VMEM((2 * O, F6), bf16),
            pltpu.VMEM((O, F6), bf16),
            pltpu.VMEM((ROWS, F6), f32),
            pltpu.VMEM((ROWS, F6), bf16),
            pltpu.VMEM((O, ROWS), bf16),
            pltpu.VMEM((ROWS, S), bf16),
            pltpu.VMEM((C, F6), bf16),
            pltpu.VMEM((768, C), bf16),
            pltpu.VMEM((F6, F6), bf16),
            pltpu.VMEM((128, 128), f32),
            pltpu.VMEM((32, 128), f32),
            pltpu.VMEM((O, C), f32),
            pltpu.VMEM((O, C), f32),
            pltpu.VMEM((3 * O, C), bf16),
            pltpu.VMEM((3 * O, C), bf16),
            pltpu.VMEM((O, C), f32),
            pltpu.VMEM((O, C), f32),
            dma((LANES,)),
            dma((LANES,)),
            dma((LANES,)),
            dma((LANES,)),
            dma((LANES,)),
            dma((LANES,)),
            dma((2, LANES)),
            dma((10,)),
            dma((10,)),
            dma((4,)),
            dma((4,)),
        ],
        compiler_params=pltpu.CompilerParams(
            collective_id=0, has_side_effects=True, vmem_limit_bytes=40 * 1024 * 1024
        ),
    )(
        jnp.transpose(positions, (1, 0, 2)),
        masses,
        block_owner.T,
        block_oct[None, :],
        jnp.transpose(face_owner, (1, 2, 0)),
        face_oct.T,
        face_coarse.T,
        face_quadrant.T,
    )
    return potential, jnp.transpose(accel, (1, 0, 2))


def solution(mesh):
    placed = (
        P("hilbert", None, None),
        P("hilbert", None),
        P("hilbert", None),
        P("hilbert"),
        P("hilbert", None, None),
        P("hilbert", None),
        P("hilbert", None),
        P("hilbert", None),
    )
    return jax.shard_map(
        on_device,
        mesh=mesh,
        in_specs=placed,
        out_specs=(P("hilbert", None), P("hilbert", None, None)),
        check_vma=False,
    )
```

time: 96.5 us -> 78.9 us (0.82)
  Pallas kernels: 88.4 us -> 73.4 us
  other arithmetic: 1.48 us -> 0 us
    pallas_call x1, Pallas kernels: 88.4 us -> 73.4 us  [on_device(): pl.pallas_call(kernel, out_shape=(jax.ShapeDtypeStruct((O, C), f32), jax....]
    concatenate x2 -> x0, other arithmetic: 1.48 us -> none  [the longest x1 0.75 us: on_device(): blocks = jnp.concatenate([block_owner, block_oct[:, None]], axis=1)]
    unnamed x11 -> x18, local copies, waits for them, and re-layouts: 4.61 us -> 4.67 us
where the time goes in v2:
time: 78.9 us; the launch traced here: 78.7 us
  Pallas kernels  73.4 us (93%)
  local copies, waits for them, and re-layouts  4.67 us (6%)
    pallas_call x1, Pallas kernels, on_device(): pl.pallas_call(kernel, out_shape=(jax.ShapeDtypeStruct((O, C), f32), jax....  73.4 us
    unnamed x18, local copies, waits for them, and re-layouts  4.67 us

profile of v2, /device:TPU:1, one launch (start us, length us, event | category | flops | bytes accessed | tf_op | source)
XLA Modules:
  0.0 78.7 jit_solution(2742429131830794153)
XLA Ops:
  0.6 0.0 copy-start.4
  0.6 0.0 copy-start.3
  0.7 0.0 copy-start.2
  0.7 0.0 copy-start.6
  0.7 0.0 copy-start.7
  0.7 0.6 copy-done.4
  1.3 0.0 copy-done.3
  1.3 0.0 copy-done.2
  1.4 0.0 copy-done.6
  1.4 0.0 copy-done.7
  1.4 0.0 copy-start
  1.4 1.0 %copy-done = f32[128,3,256]{2,0,1:T(8,128)S(1)} copy-done((f32[128,3,256]{2,0,1:T(8,128)S(1)}, f32[128,3,256]{2,0,1:T(8,128)}, u32[]{:S(2)}) %copy-start) | copy-done | bytes 393240
  2.4 0.0 copy-start.1
  2.4 0.9 %copy-done.1 = f32[128,256]{1,0:T(8,128)S(1)} copy-done((f32[128,256]{1,0:T(8,128)S(1)}, f32[128,256]{1,0:T(8,128)}, u32[]{:S(2)}) %copy-start.1) | copy-done | bytes 131096
  3.3 0.0 copy-start.5
  3.3 0.7 copy-done.5
  3.9 73.4 %shard_map.95 = (f32[64,512]{1,0:T(8,128)S(1)}, f32[3,128,256]{2,1,0:T(8,128)S(1)}) custom-call(f32[3,128,256]{2,1,0:T(8,128)S(1)} %bitcast.9, f32[128,256]{1,0:T(8,128)S(1)} %copy-done.1, s32[1,128]{1,0:T(1,128)S(1)} %bitcast.14, s32[1,128]{1,0:T(1,128)S(1)} %bitcast.15, s32[6,1,64]{2,1,0:T(1,128)S(1)} %bitcast.13, s32[6,64]{1,0:T(8,128)S(1)} %bitcast.10, ...), custom_call_target="tpu_custom_call" | custom-call | tf_op jit(solution)/shard_map/pallas_call | solution.py:452
  77.3 0.7 copy.12
  78.0 0.7 copy.13
Async XLA Ops:
  0.6 0.7 copy-start.4
  0.6 0.7 copy-start.3
  0.7 0.7 copy-start.2
  0.7 0.7 copy-start.6
  0.7 0.7 copy-start.7
  1.4 1.0 %copy-start = (f32[128,3,256]{2,0,1:T(8,128)S(1)}, f32[128,3,256]{2,0,1:T(8,128)}, u32[]{:S(2)}) copy-start(f32[128,3,256]{2,0,1:T(8,128)} %param.8) | copy-start | bytes 1179652
  2.4 0.9 %copy-start.1 = (f32[128,256]{1,0:T(8,128)S(1)}, f32[128,256]{1,0:T(8,128)}, u32[]{:S(2)}) copy-start(f32[128,256]{1,0:T(8,128)} %mass_ref.1) | copy-start | bytes 393220
  3.3 0.7 copy-start.5

commit v3 on v2

--- a/solution.py
+++ b/solution.py
@@ -90,13 +90,13 @@
 
 
 def kernel(
-    pos_ref, mass_ref, bown_ref, boct_ref, fown_ref, foct_ref, fco_ref, fq_ref,
+    pos_hbm, mass_hbm, bown_ref, boct_ref, fown_ref, foct_ref, fco_ref, fq_ref,
     phi_ref, accel_ref,
     dep_ref, req_send, req_got, msg_send, dep_got, field_got, face_send, face_got,
     sum_send, sum_got, field_ref, dens_ref, m0_ref, mc_ref, home_ref, fmask_ref, smask_ref, gro_ref, os_ref,
     pick_ref, place_ref, diag_ref, index_ref, index_got, home_send, home_got, fhome_send, fhome_got,
-    work_ref, phi_got,
-    req_ss, req_rs, msg_ss, dep_rs, field_rs, face_ss, face_rs, sum_ss, sum_rs, one_ss, one_rs,
+    work_ref, phi_got, pos_ref, mass_ref, cross_ref, homelo_send, homelo_got,
+    req_ss, req_rs, msg_ss, dep_rs, field_rs, face_ss, face_rs, sum_ss, sum_rs, one_ss, one_rs, load_sem,
 ):
     me = lax.axis_index("hilbert")
     owner = hosted_by(me)
@@ -118,6 +118,13 @@
     for p in partners:
         pl.semaphore_signal(barrier, inc=1, device_id=(p,), device_id_type=pl.DeviceIdType.MESH)
 
+    loads = [
+        pltpu.make_async_copy(mass_hbm, mass_ref, load_sem.at[0]),
+        pltpu.make_async_copy(pos_hbm, pos_ref, load_sem.at[1]),
+    ]
+    for copy in loads:
+        copy.start()
+
     def send(src, dst, ss, rs, p):
         copy = pltpu.make_async_remote_copy(
             src_ref=src, dst_ref=dst, send_sem=ss, recv_sem=rs,
@@ -186,6 +193,8 @@
     req_send[:, 0:128] = dot_t(takes.astype(bf16), wanted).astype(bf16)
     req_send[:, 128:256] = dot_t(into[0] + into[1] + into[2], oct_hot).astype(bf16)
 
+    for copy in loads:
+        copy.wait()
     masses = mass_ref[...]
     tile = masses[0:8, 0:128]
     for r in range(16):
@@ -206,9 +215,36 @@
                 left, right, (((1,), (1,)), ((), ())), preferred_element_type=f32
             )
             dep_ref[pl.ds(pl.multiple_of(i * 64 + 8 * r, 8), 8), :] = both[0:8] + both[8:16]
+            cross_ref[pl.ds(pl.multiple_of(i * 1024 + 128 * r, 128), 128), :] = right
         return carry
 
-    lax.fori_loop(0, B // 8, deposit, 0)
+    lax.fori_loop(0, B // 16, deposit, 0)
+
+    pl.semaphore_wait(barrier, len(partners))
+
+    requests = send_lanes(req_send, req_got, req_ss, req_rs, hosts)
+    index_copy = send(index_ref.at[pl.ds(0, 32)], index_got, one_ss.at[0], one_rs.at[0], my_host)
+    sums = []
+
+    def sum_start(s, tile):
+        sum_send[s] = tile
+        for j, (p, back) in enumerate(stages[s]):
+            at = first_sum[s]
+            sums.append(
+                send(sum_send.at[s], sum_got.at[at + back], sum_ss.at[at + j], sum_rs.at[at + back], p)
+            )
+
+    def sum_end(s, tile):
+        at, count = first_sum[s], len(stages[s])
+        for copy in sums[at : at + count]:
+            copy.wait_recv()
+        for j in range(count):
+            tile = tile + sum_got[at + j]
+        return tile
+
+    sum_start(0, tile)
+
+    lax.fori_loop(B // 16, B // 8, deposit, 0)
 
     low_half = iota((B, 128), 1) < S
     parts = []
@@ -225,34 +261,13 @@
         rest = rest - piece.astype(f32)
         pieces.append(piece)
     stacked = jnp.concatenate(pieces, axis=0)
-    home_send[...] = dot_t(jnp.concatenate([at_home] * 3, axis=0), stacked)[0:O]
     msg_send[...] = dot_t(jnp.concatenate(into, axis=0), stacked).astype(bf16)
-
-    pl.semaphore_wait(barrier, len(partners))
-
-    index_copy = send(index_ref.at[pl.ds(0, 32)], index_got, one_ss.at[0], one_rs.at[0], my_host)
+    deposits = send_lanes(msg_send, dep_got, msg_ss, dep_rs, hosts)
+    home = dot_t(jnp.concatenate([at_home] * 3, axis=0), stacked)[0:O]
+    home_send[...] = home.astype(bf16)
     home_copy = send(home_send, home_got, one_ss.at[1], one_rs.at[1], my_host)
-    deposits = send_lanes(msg_send, dep_got, msg_ss, dep_rs, hosts)
-    requests = send_lanes(req_send, req_got, req_ss, req_rs, hosts)
-    sums = []
-
-    def sum_start(s, tile):
-        sum_send[s] = tile
-        for j, (p, back) in enumerate(stages[s]):
-            at = first_sum[s]
-            sums.append(
-                send(sum_send.at[s], sum_got.at[at + back], sum_ss.at[at + j], sum_rs.at[at + back], p)
-            )
-
-    def sum_end(s, tile):
-        at, count = first_sum[s], len(stages[s])
-        for copy in sums[at : at + count]:
-            copy.wait_recv()
-        for j in range(count):
-            tile = tile + sum_got[at + j]
-        return tile
-
-    sum_start(0, tile)
+    homelo_send[...] = (home - home.astype(bf16).astype(f32)).astype(bf16)
+    homelo_copy = send(homelo_send, homelo_got, one_ss.at[4], one_rs.at[4], my_host)
 
     for d in range(3):
         pick_ref[:, 128 * d : 128 * d + 128] = pick_table(d)
@@ -302,7 +317,7 @@
         copy.wait_recv()
     density = dot_t(slot_octs, dep_got[...])
     home_copy.wait_recv()
-    source = COUPLING * (density + home_got[...])
+    source = COUPLING * (density + home_got[...].astype(f32))
     dens_ref[...] = source
     work_ref[...] = source * (-1.0 / 6.0)
 
@@ -347,9 +362,9 @@
         return dot(gro_ref[...], jnp.concatenate([got] * 3, axis=1) * smask_ref[...]).astype(bf16)
 
     def sweep(slot, between):
+        high, layers, copies = exchange_start(work_ref[...], slot)
+        between()
         phi = work_ref[...]
-        high, layers, copies = exchange_start(phi, slot)
-        between()
         raw = home_ghosts(phi, high, layers)
         total = placed(raw, 0, None) + placed(raw, 1, None) + placed(raw, 2, None)
         total = total[0:O] + total[O : 2 * O] - dens_ref[...]
@@ -371,8 +386,16 @@
         if s < 3:
             sum_start(s + 1, tiles[-1])
 
-    for k in range(1, 4):
-        sweep(k % 2, lambda: step_sum(k))
+    def add_low():
+        homelo_copy.wait_recv()
+        low = COUPLING * homelo_got[...].astype(f32)
+        dens_ref[...] = dens_ref[...] + low
+        work_ref[...] = work_ref[...] - low * (1.0 / 6.0)
+        step_sum(1)
+
+    sweep(1, add_low)
+    sweep(0, lambda: step_sum(2))
+    sweep(1, lambda: step_sum(3))
     total = jnp.sum(jnp.sum(tiles[-1], axis=0, keepdims=True), axis=1, keepdims=True)
     mean = total * (COUPLING / TOTAL_CELLS)
     work_ref[...] = work_ref[...] + mean * (4.0 / 6.0)
@@ -424,14 +447,14 @@
 
     def interpolate(i, carry):
         rows = pl.ds(pl.multiple_of(i * 8, 8), 8)
-        xs, ys, zs = pos_ref[0, rows, :], pos_ref[1, rows, :], pos_ref[2, rows, :]
+        xs = pos_ref[0, rows, :]
         out = [[], [], []]
         for r in range(8):
             wx = weights(xs[r : r + 1])
-            high, low = crossed(weights(ys[r : r + 1]), weights(zs[r : r + 1]))
+            both = cross_ref[pl.ds(pl.multiple_of(i * 1024 + 128 * r, 128), 128), :]
             at = pl.ds(pl.multiple_of(i * 64 + 8 * r, 8), 8)
             left = jnp.concatenate([field_ref[d, at, :] for d in range(3)], axis=0).astype(bf16)
-            value = dot(left, jnp.concatenate([high, low], axis=0))
+            value = dot(left, both)
             for d in range(3):
                 out[d].append(jnp.sum(value[8 * d : 8 * d + 8] * wx, axis=0, keepdims=True))
         for d in range(3):
@@ -440,7 +463,7 @@
 
     lax.fori_loop(0, B // 8, interpolate, 0)
 
-    for copy in [index_copy, home_copy, phi_copy, fhome_copy] + requests + sums + copies + returns:
+    for copy in [index_copy, home_copy, homelo_copy, phi_copy, fhome_copy] + requests + sums + copies + returns:
         copy.wait_send()
 
 
@@ -455,7 +478,7 @@
             jax.ShapeDtypeStruct((O, C), f32),
             jax.ShapeDtypeStruct((3, B, PART), f32),
         ),
-        in_specs=[vmem] * 8,
+        in_specs=[pl.BlockSpec(memory_space=pl.ANY)] * 2 + [vmem] * 6,
         out_specs=(vmem, vmem),
         scratch_shapes=[
             pltpu.VMEM((B * 8, 128), f32),
@@ -482,12 +505,17 @@
             pltpu.VMEM((F6, F6), bf16),
             pltpu.VMEM((128, 128), f32),
             pltpu.VMEM((32, 128), f32),
-            pltpu.VMEM((O, C), f32),
-            pltpu.VMEM((O, C), f32),
+            pltpu.VMEM((O, C), bf16),
+            pltpu.VMEM((O, C), bf16),
             pltpu.VMEM((3 * O, C), bf16),
             pltpu.VMEM((3 * O, C), bf16),
             pltpu.VMEM((O, C), f32),
             pltpu.VMEM((O, C), f32),
+            pltpu.VMEM((3, B, PART), f32),
+            pltpu.VMEM((B, PART), f32),
+            pltpu.VMEM((B * 128, PART), bf16),
+            pltpu.VMEM((O, C), bf16),
+            pltpu.VMEM((O, C), bf16),
             dma((LANES,)),
             dma((LANES,)),
             dma((LANES,)),
@@ -497,8 +525,9 @@
             dma((2, LANES)),
             dma((10,)),
             dma((10,)),
-            dma((4,)),
-            dma((4,)),
+            dma((5,)),
+            dma((5,)),
+            dma((2,)),
         ],
         compiler_params=pltpu.CompilerParams(
             collective_id=0, has_side_effects=True, vmem_limit_bytes=40 * 1024 * 1024

time: 78.9 us -> 76 us (0.963)
  Pallas kernels: 73.4 us -> 70.1 us
    pallas_call x1, Pallas kernels: 73.4 us -> 70.1 us  [on_device(): pl.pallas_call(kernel, out_shape=(jax.ShapeDtypeStruct((O, C), f32), jax....]
where the time goes in v3:
time: 76 us; the launch traced here: 75.5 us
  Pallas kernels  70.1 us (92%)
  local copies, waits for them, and re-layouts  4.67 us (6%)
    pallas_call x1, Pallas kernels, on_device(): pl.pallas_call(kernel, out_shape=(jax.ShapeDtypeStruct((O, C), f32), jax....  70.1 us
    unnamed x18, local copies, waits for them, and re-layouts  4.67 us

profile of v3, /device:TPU:1, one launch (start us, length us, event | category | flops | bytes accessed | tf_op | source)
XLA Modules:
  0.0 75.5 jit_solution(7113003372383034922)
XLA Ops:
  0.6 0.0 copy-start.4
  0.6 0.0 copy-start.3
  0.7 0.0 copy-start.2
  0.7 0.0 copy-start.6
  0.7 0.0 copy-start.7
  0.7 0.6 copy-done.4
  1.3 0.0 copy-done.3
  1.3 0.0 copy-done.2
  1.4 0.0 copy-done.6
  1.4 0.0 copy-done.7
  1.4 0.0 copy-start
  1.4 1.0 %copy-done = f32[128,3,256]{2,0,1:T(8,128)S(1)} copy-done((f32[128,3,256]{2,0,1:T(8,128)S(1)}, f32[128,3,256]{2,0,1:T(8,128)}, u32[]{:S(2)}) %copy-start) | copy-done | bytes 393240
  2.4 0.0 copy-start.1
  2.4 0.9 %copy-done.1 = f32[128,256]{1,0:T(8,128)S(1)} copy-done((f32[128,256]{1,0:T(8,128)S(1)}, f32[128,256]{1,0:T(8,128)}, u32[]{:S(2)}) %copy-start.1) | copy-done | bytes 131096
  3.3 0.0 copy-start.5
  3.3 0.7 copy-done.5
  3.9 70.1 %shard_map.95 = (f32[64,512]{1,0:T(8,128)S(1)}, f32[3,128,256]{2,1,0:T(8,128)S(1)}) custom-call(f32[3,128,256]{2,1,0:T(8,128)S(1)} %bitcast.9, f32[128,256]{1,0:T(8,128)S(1)} %copy-done.1, s32[1,128]{1,0:T(1,128)S(1)} %bitcast.14, s32[1,128]{1,0:T(1,128)S(1)} %bitcast.15, s32[6,1,64]{2,1,0:T(1,128)S(1)} %bitcast.13, s32[6,64]{1,0:T(8,128)S(1)} %bitcast.10, ...), custom_call_target="tpu_custom_call" | custom-call | tf_op jit(solution)/shard_map/pallas_call | solution.py:475
  74.1 0.7 copy.12
  74.7 0.7 copy.13
Async XLA Ops:
  0.6 0.7 copy-start.4
  0.6 0.7 copy-start.3
  0.7 0.7 copy-start.2
  0.7 0.7 copy-start.6
  0.7 0.7 copy-start.7
  1.4 1.0 %copy-start = (f32[128,3,256]{2,0,1:T(8,128)S(1)}, f32[128,3,256]{2,0,1:T(8,128)}, u32[]{:S(2)}) copy-start(f32[128,3,256]{2,0,1:T(8,128)} %param.8) | copy-start | bytes 1179652
  2.4 0.9 %copy-start.1 = (f32[128,256]{1,0:T(8,128)S(1)}, f32[128,256]{1,0:T(8,128)}, u32[]{:S(2)}) copy-start(f32[128,256]{1,0:T(8,128)} %mass_hbm.1) | copy-start | bytes 393220
  3.3 0.7 copy-start.5

commit v4 on v3

--- a/solution.py
+++ b/solution.py
@@ -94,7 +94,7 @@
     phi_ref, accel_ref,
     dep_ref, req_send, req_got, msg_send, dep_got, field_got, face_send, face_got,
     sum_send, sum_got, field_ref, dens_ref, m0_ref, mc_ref, home_ref, fmask_ref, smask_ref, gro_ref, os_ref,
-    pick_ref, place_ref, diag_ref, index_ref, index_got, home_send, home_got, fhome_send, fhome_got,
+    pick_ref, place_ref, diag_ref, index_ref, index_got, home_send, home_got, layers_got,
     work_ref, phi_got, pos_ref, mass_ref, cross_ref, homelo_send, homelo_got,
     req_ss, req_rs, msg_ss, dep_rs, field_rs, face_ss, face_rs, sum_ss, sum_rs, one_ss, one_rs, load_sem,
 ):
@@ -164,6 +164,32 @@
             [(delta[:, f : f + 1] == offs_row).astype(f32) for f in range(6)], axis=0
         )
         return (slots_of(match) == iota((F6, ROWS), 1).astype(f32)).astype(f32)
+
+    def set_tables(role, columns, of):
+        group = iota((O, F6), 1) // S
+        inside = iota((O, F6), 1) % S
+
+        def spread(base):
+            total = jnp.zeros((O, F6), i32)
+            for f in range(6):
+                total = jnp.where(group == f, columns[0:O, base + f : base + f + 1], total)
+            return total
+
+        takes = face_slots(columns, of)
+        gro = takes[0:O]
+        for f in range(1, 6):
+            gro = gro + takes[f * O : (f + 1) * O]
+        gro_ref[role] = gro.astype(bf16)
+        same_face = (iota((F6, F6), 0) // O == iota((F6, F6), 1) // S).astype(f32).astype(bf16)
+        smask_ref[role] = dot_t(takes.astype(bf16), same_face).astype(bf16)
+        home_ref[role] = ((spread(0) == of) & (spread(8) == inside)).astype(f32).astype(bf16)
+        coarse_x = spread(16)
+        quad_x = spread(24)
+        quad_in = (inside // 32) * 2 + (inside % 8) // 4
+        m0 = (coarse_x != 1).astype(f32).astype(bf16)
+        mc = ((coarse_x == 1) & (quad_x == quad_in)).astype(f32).astype(bf16)
+        m0_ref[role] = jnp.concatenate([m0, m0], axis=0)
+        mc_ref[role] = jnp.concatenate([mc, mc], axis=0)
 
     index_ref[...] = jnp.zeros((128, 128), f32)
     for f in range(6):
@@ -281,30 +307,7 @@
     index_copy.wait_recv()
     spare = jnp.zeros((96, 128), f32)
     columns = jnp.concatenate([index_got[...], spare], axis=0).T.astype(i32)
-    group = iota((O, F6), 1) // S
-
-    def spread(base):
-        total = jnp.zeros((O, F6), i32)
-        for f in range(6):
-            total = jnp.where(group == f, columns[0:O, base + f : base + f + 1], total)
-        return total
-
-    takes = face_slots(columns, owner)
-    gro = takes[0:O]
-    for f in range(1, 6):
-        gro = gro + takes[f * O : (f + 1) * O]
-    gro_ref[...] = gro.astype(bf16)
-    same_face = (iota((F6, F6), 0) // O == iota((F6, F6), 1) // S).astype(f32).astype(bf16)
-    smask_ref[...] = dot_t(takes.astype(bf16), same_face).astype(bf16)
-    inside = iota((O, F6), 1) % S
-    home_ref[...] = ((spread(0) == owner) & (spread(8) == inside)).astype(f32).astype(bf16)
-    coarse_x = spread(16)
-    quad_x = spread(24)
-    quad_in = (inside // 32) * 2 + (inside % 8) // 4
-    m0 = (coarse_x != 1).astype(f32).astype(bf16)
-    mc = ((coarse_x == 1) & (quad_x == quad_in)).astype(f32).astype(bf16)
-    m0_ref[...] = jnp.concatenate([m0, m0], axis=0)
-    mc_ref[...] = jnp.concatenate([mc, mc], axis=0)
+    set_tables(0, columns, owner)
 
     for copy in requests:
         copy.wait_recv()
@@ -330,13 +333,16 @@
         down = jnp.where(at[d] > 0, pltpu.roll(phi, strides[d], 1), 0.0)
         return up, down
 
-    def placed(raw, d, sign):
+    def placed(raw, d, sign=None, role=0):
         rows = raw.shape[0]
         part = raw[:, 128 * d : 128 * d + 128]
         if sign is not None:
             part = part * sign
         left = jnp.concatenate(
-            [part * m0_ref[0:rows, 128 * d : 128 * d + 128], part * mc_ref[0:rows, 128 * d : 128 * d + 128]],
+            [
+                part * m0_ref[role, 0:rows, 128 * d : 128 * d + 128],
+                part * mc_ref[role, 0:rows, 128 * d : 128 * d + 128],
+            ],
             axis=1,
         )
         return dot(left, place_ref[256 * d : 256 * d + 256, :])
@@ -350,31 +356,31 @@
         copies = send_lanes(face_send, face_got.at[slot], face_ss, face_rs.at[slot], peers)
         return high, layers, copies
 
-    def home_ghosts(phi, high, layers):
+    def home_ghosts(phi, high, layers, role=0):
         low = (phi - high.astype(f32)).astype(bf16)
         layers_low = dot(low, pick_ref[...]).astype(bf16)
         diag = diag_ref[...]
         wide = [jnp.concatenate([x] * 6, axis=0) * diag for x in (layers, layers_low)]
-        return jnp.concatenate([dot(home_ref[...], x).astype(bf16) for x in wide], axis=0)
-
-    def away_ghosts(slot):
-        got = face_got[slot]
-        return dot(gro_ref[...], jnp.concatenate([got] * 3, axis=1) * smask_ref[...]).astype(bf16)
+        return jnp.concatenate([dot(home_ref[role], x).astype(bf16) for x in wide], axis=0)
+
+    def away_ghosts(got, role=0):
+        wide = jnp.concatenate([got] * 3, axis=1) * smask_ref[role]
+        return dot(gro_ref[role], wide).astype(bf16)
 
     def sweep(slot, between):
         high, layers, copies = exchange_start(work_ref[...], slot)
         between()
         phi = work_ref[...]
         raw = home_ghosts(phi, high, layers)
-        total = placed(raw, 0, None) + placed(raw, 1, None) + placed(raw, 2, None)
+        total = placed(raw, 0) + placed(raw, 1) + placed(raw, 2)
         total = total[0:O] + total[O : 2 * O] - dens_ref[...]
         for d in range(3):
             up, down = inner(phi, d)
             total = total + (up + down)
         for copy in copies:
             copy.wait_recv()
-        raw = away_ghosts(slot)
-        total = total + (placed(raw, 0, None) + placed(raw, 1, None) + placed(raw, 2, None))
+        raw = away_ghosts(face_got[slot])
+        total = total + (placed(raw, 0) + placed(raw, 1) + placed(raw, 2))
         work_ref[...] = total * (1.0 / 6.0)
         for copy in copies:
             copy.wait_send()
@@ -394,7 +400,11 @@
         step_sum(1)
 
     sweep(1, add_low)
-    sweep(0, lambda: step_sum(2))
+    def own_tables():
+        step_sum(2)
+        set_tables(1, index_ref[...].T.astype(i32), me)
+
+    sweep(0, own_tables)
     sweep(1, lambda: step_sum(3))
     total = jnp.sum(jnp.sum(tiles[-1], axis=0, keepdims=True), axis=1, keepdims=True)
     mean = total * (COUPLING / TOTAL_CELLS)
@@ -413,32 +423,45 @@
     high, layers, copies = exchange_start(phi, 0)
     phi_copy = send(work_ref, phi_got, one_ss.at[3], one_rs.at[3], owner)
     sign = jnp.where(iota((1, 128), 1) < S, 0.5, -0.5).astype(bf16)
-    raw = home_ghosts(phi, high, layers)
-    local = []
-    for d in range(3):
-        up, down = inner(phi, d)
-        part = placed(raw, d, sign)
-        local.append(0.5 * (down - up) + part[0:O] + part[O : 2 * O])
+
+    def near_field(phi, high, layers, role):
+        raw = home_ghosts(phi, high, layers, role)
+        parts = []
+        for d in range(3):
+            up, down = inner(phi, d)
+            part = placed(raw, d, sign, role)
+            parts.append(0.5 * (down - up) + part[0:O] + part[O : 2 * O])
+        return parts
+
+    def whole_field(local, got, role):
+        raw = away_ghosts(got, role)
+        return [(local[d] + placed(raw, d, sign, role)).astype(bf16) for d in range(3)]
+
+    local = near_field(phi, high, layers, 0)
     for copy in copies:
         copy.wait_recv()
-    raw = away_ghosts(0)
-    field = [(local[d] + placed(raw, d, sign)).astype(bf16) for d in range(3)]
-    fhome_send[...] = jnp.concatenate(field, axis=0)
-    fhome_copy = send(fhome_send, fhome_got, one_ss.at[2], one_rs.at[2], owner)
+    layers_copy = send(face_got.at[0], layers_got, one_ss.at[2], one_rs.at[2], owner)
+    field = whole_field(local, face_got[0], 0)
     row_dim = iota((ROWS, 1), 0) % 16 // 4
     picked = [dot(slot_octs, field[d]) for d in range(3)]
     msg_send[...] = jnp.where(
         row_dim == 0, picked[0], jnp.where(row_dim == 1, picked[1], picked[2])
     ).astype(bf16)
     returns = send_lanes(msg_send, field_got, msg_ss, field_rs, holders)
+
     phi_copy.wait_recv()
-    phi_ref[...] = phi_got[...]
-    fhome_copy.wait_recv()
+    own = phi_got[...]
+    phi_ref[...] = own
+    high = own.astype(bf16)
+    local = near_field(own, high, dot(high, pick_ref[...]).astype(bf16), 1)
+    layers_copy.wait_recv()
+    field = whole_field(local, layers_got[...], 1)
+    mine = [dot(at_home[:, 0:O], field[d]) for d in range(3)]
     for copy in returns:
         copy.wait_recv()
     got = field_got[...]
     for d in range(3):
-        values = dot(at_home[:, 0:O], fhome_got[O * d : O * d + O]) + dot(into[d], got)
+        values = mine[d] + dot(into[d], got)
         for i in range(4):
             pair = values[:, 128 * i : 128 * i + 128]
             turned = pltpu.roll(pair, S, 1)
@@ -463,7 +486,7 @@
 
     lax.fori_loop(0, B // 8, interpolate, 0)
 
-    for copy in [index_copy, home_copy, homelo_copy, phi_copy, fhome_copy] + requests + sums + copies + returns:
+    for copy in [index_copy, home_copy, homelo_copy, phi_copy, layers_copy] + requests + sums + copies + returns:
         copy.wait_send()
 
 
@@ -493,12 +516,12 @@
             pltpu.VMEM((10, 8, 128), f32),
             pltpu.VMEM((3, B * 8, 128), f32),
             pltpu.VMEM((O, C), f32),
-            pltpu.VMEM((2 * O, F6), bf16),
-            pltpu.VMEM((2 * O, F6), bf16),
-            pltpu.VMEM((O, F6), bf16),
+            pltpu.VMEM((2, 2 * O, F6), bf16),
+            pltpu.VMEM((2, 2 * O, F6), bf16),
+            pltpu.VMEM((2, O, F6), bf16),
             pltpu.VMEM((ROWS, F6), f32),
-            pltpu.VMEM((ROWS, F6), bf16),
-            pltpu.VMEM((O, ROWS), bf16),
+            pltpu.VMEM((2, ROWS, F6), bf16),
+            pltpu.VMEM((2, O, ROWS), bf16),
             pltpu.VMEM((ROWS, S), bf16),
             pltpu.VMEM((C, F6), bf16),
             pltpu.VMEM((768, C), bf16),
@@ -507,8 +530,7 @@
             pltpu.VMEM((32, 128), f32),
             pltpu.VMEM((O, C), bf16),
             pltpu.VMEM((O, C), bf16),
-            pltpu.VMEM((3 * O, C), bf16),
-            pltpu.VMEM((3 * O, C), bf16),
+            pltpu.VMEM((ROWS, 128), bf16),
             pltpu.VMEM((O, C), f32),
             pltpu.VMEM((O, C), f32),
             pltpu.VMEM((3, B, PART), f32),
@@ -530,7 +552,7 @@
             dma((2,)),
         ],
         compiler_params=pltpu.CompilerParams(
-            collective_id=0, has_side_effects=True, vmem_limit_bytes=40 * 1024 * 1024
+            collective_id=0, has_side_effects=True, vmem_limit_bytes=56 * 1024 * 1024
         ),
     )(
         jnp.transpose(positions, (1, 0, 2)),

time: 76 us -> 71.9 us (0.946)
  Pallas kernels: 70.1 us -> 67.4 us
  local copies, waits for them, and re-layouts: 4.67 us -> 3.33 us
    pallas_call x1, Pallas kernels: 70.1 us -> 67.4 us  [on_device(): pl.pallas_call(kernel, out_shape=(jax.ShapeDtypeStruct((O, C), f32), jax....]
    unnamed x18 -> x2, local copies, waits for them, and re-layouts: 4.67 us -> 3.33 us
where the time goes in v4:
time: 71.9 us; the launch traced here: 71.4 us
  Pallas kernels  67.4 us (94%)
  local copies, waits for them, and re-layouts  3.33 us (5%)
    pallas_call x1, Pallas kernels, on_device(): pl.pallas_call(kernel, out_shape=(jax.ShapeDtypeStruct((O, C), f32), jax....  67.4 us
    unnamed x2, local copies, waits for them, and re-layouts  3.33 us

profile of v4, /device:TPU:1, one launch (start us, length us, event | category | flops | bytes accessed | tf_op | source)
XLA Modules:
  0.0 71.4 jit_solution(16944324408295797827)
XLA Ops:
  0.6 67.4 %shard_map.95 = (f32[64,512]{1,0:T(8,128)}, f32[3,128,256]{2,1,0:T(8,128)}) custom-call(f32[3,128,256]{2,1,0:T(8,128)} %bitcast.9, f32[128,256]{1,0:T(8,128)} %mass_hbm.1, s32[1,128]{1,0:T(1,128)} %bitcast.14, s32[1,128]{1,0:T(1,128)} %bitcast.15, s32[6,1,64]{2,1,0:T(1,128)} %bitcast.13, s32[6,64]{1,0:T(8,128)} %bitcast.10, s32[6,64]{1,0:T(8,128)} %bitcast.11, ...), custom_call_target="tpu_custom_call" | custom-call | tf_op jit(solution)/shard_map/pallas_call | solution.py:498
  68.1 1.6 %copy.12 = f32[64,512]{1,0:T(8,128)} copy(f32[64,512]{1,0:T(8,128)} %get-tuple-element.8) | data formatting | bytes 262144
  69.6 1.8 %copy.13 = f32[128,3,256]{2,0,1:T(8,128)} copy(f32[128,3,256]{2,0,1:T(8,128)} %bitcast.8) | data formatting | bytes 786432

commit v5 on v4

--- a/solution.py
+++ b/solution.py
@@ -96,6 +96,7 @@
     sum_send, sum_got, field_ref, dens_ref, m0_ref, mc_ref, home_ref, fmask_ref, smask_ref, gro_ref, os_ref,
     pick_ref, place_ref, diag_ref, index_ref, index_got, home_send, home_got, layers_got,
     work_ref, phi_got, pos_ref, mass_ref, cross_ref, homelo_send, homelo_got,
+    slots_ref, m0s_ref, mcs_ref, next_ref,
     req_ss, req_rs, msg_ss, dep_rs, field_rs, face_ss, face_rs, sum_ss, sum_rs, one_ss, one_rs, load_sem,
 ):
     me = lax.axis_index("hilbert")
@@ -298,6 +299,9 @@
     for d in range(3):
         pick_ref[:, 128 * d : 128 * d + 128] = pick_table(d)
         place_ref[256 * d : 256 * d + 256, :] = place_table(d)
+    for d in range(3):
+        rows = slice(256 * d, 256 * d + 256)
+        next_ref[rows, :] = dot(place_ref[rows, :], pick_ref[...]).astype(bf16)
     diag_ref[...] = (iota((F6, F6), 0) // S == iota((F6, F6), 1) // S).astype(f32).astype(bf16)
     to_face = (iota((128, F6), 0) - S == iota((128, F6), 1) // S).astype(f32).astype(bf16)
 
@@ -347,43 +351,71 @@
         )
         return dot(left, place_ref[256 * d : 256 * d + 256, :])
 
-    def exchange_start(phi, slot):
-        high = phi.astype(bf16)
-        layers = dot(high, pick_ref[...]).astype(bf16)
-        chosen = dot(os_ref[...], layers) * fmask_ref[...]
+    def face_copies(slot):
+        return [
+            pltpu.make_async_remote_copy(
+                src_ref=face_send.at[pl.ds(16 * l, 16)],
+                dst_ref=face_got.at[slot, pl.ds(16 * BACK[l], 16)],
+                send_sem=face_ss.at[l], recv_sem=face_rs.at[slot, BACK[l]],
+                device_id=(peers[l],), device_id_type=pl.DeviceIdType.MESH,
+            )
+            for l in LANE_ORDER
+        ]
+
+    def send_faces(chosen, slot):
+        chosen = chosen * fmask_ref[...]
         out = chosen[:, 0:128] + chosen[:, 128:256] + chosen[:, 256:384]
         face_send[...] = (out + pltpu.roll(out, S, 1)).astype(bf16)
-        copies = send_lanes(face_send, face_got.at[slot], face_ss, face_rs.at[slot], peers)
-        return high, layers, copies
-
-    def home_ghosts(phi, high, layers, role=0):
-        low = (phi - high.astype(f32)).astype(bf16)
-        layers_low = dot(low, pick_ref[...]).astype(bf16)
+        for copy in face_copies(slot):
+            copy.start()
+
+    def layers_of(values):
+        high = values.astype(bf16)
+        low = (values - high.astype(f32)).astype(bf16)
+        return [dot(x, pick_ref[...]).astype(bf16) for x in (high, low)]
+
+    def home_ghosts(layers, role=0):
         diag = diag_ref[...]
-        wide = [jnp.concatenate([x] * 6, axis=0) * diag for x in (layers, layers_low)]
+        wide = [jnp.concatenate([x] * 6, axis=0) * diag for x in layers]
         return jnp.concatenate([dot(home_ref[role], x).astype(bf16) for x in wide], axis=0)
+
+    def both_masks(part, d, fine, coarse):
+        cols = slice(128 * d, 128 * d + 128)
+        return jnp.concatenate([part * fine[:, cols], part * coarse[:, cols]], axis=1)
 
     def away_ghosts(got, role=0):
         wide = jnp.concatenate([got] * 3, axis=1) * smask_ref[role]
         return dot(gro_ref[role], wide).astype(bf16)
 
-    def sweep(slot, between):
-        high, layers, copies = exchange_start(work_ref[...], slot)
+    def sweep(slot, later_slot, between, shift=None):
         between()
         phi = work_ref[...]
-        raw = home_ghosts(phi, high, layers)
+        raw = home_ghosts(layers_of(phi))
         total = placed(raw, 0) + placed(raw, 1) + placed(raw, 2)
         total = total[0:O] + total[O : 2 * O] - dens_ref[...]
         for d in range(3):
             up, down = inner(phi, d)
             total = total + (up + down)
+        parts = layers_of(total)
+        chosen = dot(os_ref[...], parts[0]) + dot(os_ref[...], parts[1])
+        copies = face_copies(slot)
         for copy in copies:
             copy.wait_recv()
-        raw = away_ghosts(face_got[slot])
+        got = face_got[slot]
+        wide = jnp.concatenate([got] * 3, axis=1) * smask_ref[0]
+        raw = dot(slots_ref[...], wide).astype(bf16)
+        for d in range(3):
+            left = both_masks(raw[:, 128 * d : 128 * d + 128], d, m0s_ref, mcs_ref)
+            chosen = chosen + dot(left, next_ref[256 * d : 256 * d + 256, :])
+        chosen = chosen * (1.0 / 6.0)
+        if shift is not None:
+            chosen = chosen + shift()
+        for copy in copies:
+            copy.wait_send()
+        send_faces(chosen, later_slot)
+        raw = away_ghosts(got)
         total = total + (placed(raw, 0) + placed(raw, 1) + placed(raw, 2))
         work_ref[...] = total * (1.0 / 6.0)
-        for copy in copies:
-            copy.wait_send()
 
     tiles = [tile]
 
@@ -391,6 +423,10 @@
         tiles.append(sum_end(s, tiles[-1]))
         if s < 3:
             sum_start(s + 1, tiles[-1])
+
+    def mean_of_all():
+        total = jnp.sum(jnp.sum(tiles[-1], axis=0, keepdims=True), axis=1, keepdims=True)
+        return total * (COUPLING / TOTAL_CELLS)
 
     def add_low():
         homelo_copy.wait_recv()
@@ -398,21 +434,25 @@
         dens_ref[...] = dens_ref[...] + low
         work_ref[...] = work_ref[...] - low * (1.0 / 6.0)
         step_sum(1)
-
-    sweep(1, add_low)
+        slots_ref[...] = dot(os_ref[...], gro_ref[0]).astype(bf16)
+        m0s_ref[...] = dot(os_ref[...], m0_ref[0, 0:O, :]).astype(bf16)
+        mcs_ref[...] = dot(os_ref[...], mc_ref[0, 0:O, :]).astype(bf16)
+
+    first = work_ref[...].astype(bf16)
+    send_faces(dot(os_ref[...], dot(first, pick_ref[...]).astype(bf16)), 1)
+    sweep(1, 2, add_low)
     def own_tables():
         step_sum(2)
         set_tables(1, index_ref[...].T.astype(i32), me)
 
-    sweep(0, own_tables)
-    sweep(1, lambda: step_sum(3))
-    total = jnp.sum(jnp.sum(tiles[-1], axis=0, keepdims=True), axis=1, keepdims=True)
-    mean = total * (COUPLING / TOTAL_CELLS)
+    sweep(2, 0, own_tables)
+    sweep(0, 1, lambda: step_sum(3), lambda: mean_of_all() * (4.0 / 6.0))
+    mean = mean_of_all()
     work_ref[...] = work_ref[...] + mean * (4.0 / 6.0)
     dens_ref[...] = dens_ref[...] - mean
 
     def later(k, carry):
-        sweep(lax.rem(k, 2), lambda: None)
+        sweep(lax.rem(k, 3), lax.rem(k + 1, 3), lambda: None)
         return carry
 
     lax.fori_loop(4, 8, later, 0)
@@ -420,12 +460,11 @@
     for copy in deposits:
         copy.wait_send()
     phi = work_ref[...]
-    high, layers, copies = exchange_start(phi, 0)
     phi_copy = send(work_ref, phi_got, one_ss.at[3], one_rs.at[3], owner)
     sign = jnp.where(iota((1, 128), 1) < S, 0.5, -0.5).astype(bf16)
 
-    def near_field(phi, high, layers, role):
-        raw = home_ghosts(phi, high, layers, role)
+    def near_field(phi, role):
+        raw = home_ghosts(layers_of(phi), role)
         parts = []
         for d in range(3):
             up, down = inner(phi, d)
@@ -437,11 +476,12 @@
         raw = away_ghosts(got, role)
         return [(local[d] + placed(raw, d, sign, role)).astype(bf16) for d in range(3)]
 
-    local = near_field(phi, high, layers, 0)
+    local = near_field(phi, 0)
+    copies = face_copies(2)
     for copy in copies:
         copy.wait_recv()
-    layers_copy = send(face_got.at[0], layers_got, one_ss.at[2], one_rs.at[2], owner)
-    field = whole_field(local, face_got[0], 0)
+    layers_copy = send(face_got.at[2], layers_got, one_ss.at[2], one_rs.at[2], owner)
+    field = whole_field(local, face_got[2], 0)
     row_dim = iota((ROWS, 1), 0) % 16 // 4
     picked = [dot(slot_octs, field[d]) for d in range(3)]
     msg_send[...] = jnp.where(
@@ -452,8 +492,7 @@
     phi_copy.wait_recv()
     own = phi_got[...]
     phi_ref[...] = own
-    high = own.astype(bf16)
-    local = near_field(own, high, dot(high, pick_ref[...]).astype(bf16), 1)
+    local = near_field(own, 1)
     layers_copy.wait_recv()
     field = whole_field(local, layers_got[...], 1)
     mine = [dot(at_home[:, 0:O], field[d]) for d in range(3)]
@@ -511,7 +550,7 @@
             pltpu.VMEM((ROWS, C), bf16),
             pltpu.VMEM((ROWS, C), bf16),
             pltpu.VMEM((ROWS, 128), bf16),
-            pltpu.VMEM((2, ROWS, 128), bf16),
+            pltpu.VMEM((3, ROWS, 128), bf16),
             pltpu.VMEM((4, 8, 128), f32),
             pltpu.VMEM((10, 8, 128), f32),
             pltpu.VMEM((3, B * 8, 128), f32),
@@ -538,13 +577,17 @@
             pltpu.VMEM((B * 128, PART), bf16),
             pltpu.VMEM((O, C), bf16),
             pltpu.VMEM((O, C), bf16),
+            pltpu.VMEM((ROWS, ROWS), bf16),
+            pltpu.VMEM((ROWS, F6), bf16),
+            pltpu.VMEM((ROWS, F6), bf16),
+            pltpu.VMEM((768, F6), bf16),
             dma((LANES,)),
             dma((LANES,)),
             dma((LANES,)),
             dma((LANES,)),
             dma((LANES,)),
             dma((LANES,)),
-            dma((2, LANES)),
+            dma((3, LANES)),
             dma((10,)),
             dma((10,)),
             dma((5,)),
@@ -552,7 +595,7 @@
             dma((2,)),
         ],
         compiler_params=pltpu.CompilerParams(
-            collective_id=0, has_side_effects=True, vmem_limit_bytes=56 * 1024 * 1024
+            collective_id=0, has_side_effects=True, vmem_limit_bytes=54528 * 1024
         ),
     )(
         jnp.transpose(positions, (1, 0, 2)),

time: 71.9 us -> 68.6 us (0.954)
  Pallas kernels: 67.4 us -> 63.8 us
    pallas_call x1, Pallas kernels: 67.4 us -> 63.8 us  [on_device(): pl.pallas_call(kernel, out_shape=(jax.ShapeDtypeStruct((O, C), f32), jax....]
    unnamed x2 -> x16, local copies, waits for them, and re-layouts: 3.33 us -> 3.68 us
where the time goes in v5:
time: 68.6 us; the launch traced here: 68.1 us
  Pallas kernels  63.8 us (93%)
  local copies, waits for them, and re-layouts  3.68 us (5%)
  between operations  0.69 us (1%)
    pallas_call x1, Pallas kernels, on_device(): pl.pallas_call(kernel, out_shape=(jax.ShapeDtypeStruct((O, C), f32), jax....  63.8 us
    unnamed x16, local copies, waits for them, and re-layouts  3.68 us

profile of v5, /device:TPU:1, one launch (start us, length us, event | category | flops | bytes accessed | tf_op | source)
XLA Modules:
  0.0 68.1 jit_solution(2684288149449575417)
XLA Ops:
  0.6 0.0 copy-start.3
  0.6 0.0 copy-start.2
  0.7 0.0 copy-start.1
  0.7 0.0 copy-start.5
  0.7 0.0 copy-start.6
  0.7 0.6 copy-done.3
  1.3 0.0 copy-done.2
  1.3 0.0 copy-done.1
  1.4 0.0 copy-done.5
  1.4 0.0 copy-done.6
  1.4 0.0 copy-start
  1.4 0.9 %copy-done = f32[128,256]{1,0:T(8,128)S(1)} copy-done((f32[128,256]{1,0:T(8,128)S(1)}, f32[128,256]{1,0:T(8,128)}, u32[]{:S(2)}) %copy-start) | copy-done | bytes 131096
  2.3 0.0 copy-start.4
  2.3 0.7 %copy-done.4 = s32[64,6,1]{0,2,1:T(1,128)S(1)} copy-done((s32[64,6,1]{0,2,1:T(1,128)S(1)}, s32[64,6,1]{0,2,1:T(1,128)}, u32[]{:S(2)}) %copy-start.4) | copy-done | bytes 1560
  2.9 63.8 %shard_map.95 = (f32[64,512]{1,0:T(8,128)S(1)}, f32[3,128,256]{2,1,0:T(8,128)S(1)}) custom-call(f32[3,128,256]{2,1,0:T(8,128)} %bitcast.15, f32[128,256]{1,0:T(8,128)S(1)} %copy-done, s32[1,128]{1,0:T(1,128)S(1)} %bitcast.13, s32[1,128]{1,0:T(1,128)S(1)} %bitcast.14, s32[6,1,64]{2,1,0:T(1,128)S(1)} %bitcast.12, s32[6,64]{1,0:T(8,128)S(1)} %bitcast.9, ...), custom_call_target="tpu_custom_call" | custom-call | tf_op jit(solution)/shard_map/pallas_call | solution.py:537
  66.7 0.7 copy.12
  67.4 0.7 %copy.13 = f32[128,3,256]{2,0,1:T(8,128)} copy(f32[128,3,256]{2,0,1:T(8,128)S(1)} %bitcast.8) | data formatting | bytes 786432
Async XLA Ops:
  0.6 0.7 %copy-start.3 = (s32[64,6]{0,1:T(8,128)S(1)}, s32[64,6]{0,1:T(8,128)}, u32[]{:S(2)}) copy-start(s32[64,6]{0,1:T(8,128)} %param.15) | copy-start | bytes 4612
  0.6 0.7 %copy-start.2 = (s32[64,6]{0,1:T(8,128)S(1)}, s32[64,6]{0,1:T(8,128)}, u32[]{:S(2)}) copy-start(s32[64,6]{0,1:T(8,128)} %param.14) | copy-start | bytes 4612
  0.7 0.7 %copy-start.1 = (s32[64,6]{0,1:T(8,128)S(1)}, s32[64,6]{0,1:T(8,128)}, u32[]{:S(2)}) copy-start(s32[64,6]{0,1:T(8,128)} %param.13) | copy-start | bytes 4612
  0.7 0.7 %copy-start.5 = (s32[128,1]{0,1:T(1,128)S(1)}, s32[128,1]{0,1:T(1,128)}, u32[]{:S(2)}) copy-start(s32[128,1]{0,1:T(1,128)} %param.10) | copy-start | bytes 1540
  0.7 0.7 %copy-start.6 = (s32[128]{0:T(128)S(1)}, s32[128]{0:T(128)}, u32[]{:S(2)}) copy-start(s32[128]{0:T(128)} %param.11) | copy-start | bytes 1540
  1.4 0.9 %copy-start = (f32[128,256]{1,0:T(8,128)S(1)}, f32[128,256]{1,0:T(8,128)}, u32[]{:S(2)}) copy-start(f32[128,256]{1,0:T(8,128)} %mass_hbm.1) | copy-start | bytes 393220
  2.3 0.7 %copy-start.4 = (s32[64,6,1]{0,2,1:T(1,128)S(1)}, s32[64,6,1]{0,2,1:T(1,128)}, u32[]{:S(2)}) copy-start(s32[64,6,1]{0,2,1:T(1,128)} %param.12) | copy-start | bytes 4612

commit v6 on v5

--- a/solution.py
+++ b/solution.py
@@ -230,9 +230,9 @@
                 tile = tile + masses[8 * r : 8 * r + 8, 128 * h : 128 * h + 128]
 
     def deposit(i, carry):
-        rows = pl.ds(pl.multiple_of(i * 8, 8), 8)
+        rows = pl.ds(pl.multiple_of(i * 32, 32), 32)
         xs, ys, zs, ms = pos_ref[0, rows, :], pos_ref[1, rows, :], pos_ref[2, rows, :], mass_ref[rows, :]
-        for r in range(8):
+        for r in range(32):
             wx = weights(xs[r : r + 1]) * ms[r : r + 1]
             high, low = crossed(weights(ys[r : r + 1]), weights(zs[r : r + 1]))
             x_high = wx.astype(bf16).astype(f32)
@@ -241,11 +241,11 @@
             both = lax.dot_general(
                 left, right, (((1,), (1,)), ((), ())), preferred_element_type=f32
             )
-            dep_ref[pl.ds(pl.multiple_of(i * 64 + 8 * r, 8), 8), :] = both[0:8] + both[8:16]
-            cross_ref[pl.ds(pl.multiple_of(i * 1024 + 128 * r, 128), 128), :] = right
+            dep_ref[pl.ds(pl.multiple_of(i * 256 + 8 * r, 8), 8), :] = both[0:8] + both[8:16]
+            cross_ref[pl.ds(pl.multiple_of(i * 4096 + 128 * r, 128), 128), :] = right
         return carry
 
-    lax.fori_loop(0, B // 16, deposit, 0)
+    lax.fori_loop(0, B // 64, deposit, 0)
 
     pl.semaphore_wait(barrier, len(partners))
 
@@ -271,7 +271,7 @@
 
     sum_start(0, tile)
 
-    lax.fori_loop(B // 16, B // 8, deposit, 0)
+    lax.fori_loop(B // 64, B // 32, deposit, 0)
 
     low_half = iota((B, 128), 1) < S
     parts = []
@@ -508,13 +508,13 @@
             field_ref[d, pl.ds(2 * i + 1, B, stride=8), :] = jnp.where(low_half, turned, pair)
 
     def interpolate(i, carry):
-        rows = pl.ds(pl.multiple_of(i * 8, 8), 8)
+        rows = pl.ds(pl.multiple_of(i * 32, 32), 32)
         xs = pos_ref[0, rows, :]
         out = [[], [], []]
-        for r in range(8):
+        for r in range(32):
             wx = weights(xs[r : r + 1])
-            both = cross_ref[pl.ds(pl.multiple_of(i * 1024 + 128 * r, 128), 128), :]
-            at = pl.ds(pl.multiple_of(i * 64 + 8 * r, 8), 8)
+            both = cross_ref[pl.ds(pl.multiple_of(i * 4096 + 128 * r, 128), 128), :]
+            at = pl.ds(pl.multiple_of(i * 256 + 8 * r, 8), 8)
             left = jnp.concatenate([field_ref[d, at, :] for d in range(3)], axis=0).astype(bf16)
             value = dot(left, both)
             for d in range(3):
@@ -523,7 +523,7 @@
             accel_ref[d, rows, :] = jnp.concatenate(out[d], axis=0)
         return carry
 
-    lax.fori_loop(0, B // 8, interpolate, 0)
+    lax.fori_loop(0, B // 32, interpolate, 0)
 
     for copy in [index_copy, home_copy, homelo_copy, phi_copy, layers_copy] + requests + sums + copies + returns:
         copy.wait_send()

time: 68.6 us -> 66.1 us (0.964)
  Pallas kernels: 63.8 us -> 60.8 us
    pallas_call x1, Pallas kernels: 63.8 us -> 60.8 us  [on_device(): pl.pallas_call(kernel, out_shape=(jax.ShapeDtypeStruct((O, C), f32), jax....]
where the time goes in v6:
time: 66.1 us; the launch traced here: 65.2 us
  Pallas kernels  60.8 us (92%)
  local copies, waits for them, and re-layouts  3.68 us (6%)
  between operations  0.69 us (1%)
    pallas_call x1, Pallas kernels, on_device(): pl.pallas_call(kernel, out_shape=(jax.ShapeDtypeStruct((O, C), f32), jax....  60.8 us
    unnamed x16, local copies, waits for them, and re-layouts  3.68 us

profile of v6, /device:TPU:1, one launch (start us, length us, event | category | flops | bytes accessed | tf_op | source)
XLA Modules:
  0.0 65.2 jit_solution(180241990291659894)
XLA Ops:
  0.6 0.0 copy-start.3
  0.6 0.0 copy-start.2
  0.7 0.0 copy-start.1
  0.7 0.0 copy-start.5
  0.7 0.0 copy-start.6
  0.7 0.6 copy-done.3
  1.3 0.0 copy-done.2
  1.3 0.0 copy-done.1
  1.4 0.0 copy-done.5
  1.4 0.0 copy-done.6
  1.4 0.0 copy-start
  1.4 0.9 %copy-done = f32[128,256]{1,0:T(8,128)S(1)} copy-done((f32[128,256]{1,0:T(8,128)S(1)}, f32[128,256]{1,0:T(8,128)}, u32[]{:S(2)}) %copy-start) | copy-done | bytes 131096
  2.3 0.0 copy-start.4
  2.3 0.7 %copy-done.4 = s32[64,6,1]{0,2,1:T(1,128)S(1)} copy-done((s32[64,6,1]{0,2,1:T(1,128)S(1)}, s32[64,6,1]{0,2,1:T(1,128)}, u32[]{:S(2)}) %copy-start.4) | copy-done | bytes 1560
  2.9 60.8 %shard_map.95 = (f32[64,512]{1,0:T(8,128)S(1)}, f32[3,128,256]{2,1,0:T(8,128)S(1)}) custom-call(f32[3,128,256]{2,1,0:T(8,128)} %bitcast.15, f32[128,256]{1,0:T(8,128)S(1)} %copy-done, s32[1,128]{1,0:T(1,128)S(1)} %bitcast.13, s32[1,128]{1,0:T(1,128)S(1)} %bitcast.14, s32[6,1,64]{2,1,0:T(1,128)S(1)} %bitcast.12, s32[6,64]{1,0:T(8,128)S(1)} %bitcast.9, ...), custom_call_target="tpu_custom_call" | custom-call | tf_op jit(solution)/shard_map/pallas_call | solution.py:537
  63.8 0.7 %copy.12 = f32[64,512]{1,0:T(8,128)} copy(f32[64,512]{1,0:T(8,128)S(1)} %get-tuple-element.8) | data formatting | bytes 262144
  64.5 0.7 %copy.13 = f32[128,3,256]{2,0,1:T(8,128)} copy(f32[128,3,256]{2,0,1:T(8,128)S(1)} %bitcast.8) | data formatting | bytes 786432
Async XLA Ops:
  0.6 0.7 %copy-start.3 = (s32[64,6]{0,1:T(8,128)S(1)}, s32[64,6]{0,1:T(8,128)}, u32[]{:S(2)}) copy-start(s32[64,6]{0,1:T(8,128)} %param.15) | copy-start | bytes 4612
  0.6 0.7 %copy-start.2 = (s32[64,6]{0,1:T(8,128)S(1)}, s32[64,6]{0,1:T(8,128)}, u32[]{:S(2)}) copy-start(s32[64,6]{0,1:T(8,128)} %param.14) | copy-start | bytes 4612
  0.7 0.7 %copy-start.1 = (s32[64,6]{0,1:T(8,128)S(1)}, s32[64,6]{0,1:T(8,128)}, u32[]{:S(2)}) copy-start(s32[64,6]{0,1:T(8,128)} %param.13) | copy-start | bytes 4612
  0.7 0.7 %copy-start.5 = (s32[128,1]{0,1:T(1,128)S(1)}, s32[128,1]{0,1:T(1,128)}, u32[]{:S(2)}) copy-start(s32[128,1]{0,1:T(1,128)} %param.10) | copy-start | bytes 1540
  0.7 0.7 %copy-start.6 = (s32[128]{0:T(128)S(1)}, s32[128]{0:T(128)}, u32[]{:S(2)}) copy-start(s32[128]{0:T(128)} %param.11) | copy-start | bytes 1540
  1.4 0.9 %copy-start = (f32[128,256]{1,0:T(8,128)S(1)}, f32[128,256]{1,0:T(8,128)}, u32[]{:S(2)}) copy-start(f32[128,256]{1,0:T(8,128)} %mass_hbm.1) | copy-start | bytes 393220
  2.3 0.7 %copy-start.4 = (s32[64,6,1]{0,2,1:T(1,128)S(1)}, s32[64,6,1]{0,2,1:T(1,128)}, u32[]{:S(2)}) copy-start(s32[64,6,1]{0,2,1:T(1,128)} %param.12) | copy-start | bytes 4612

commit v7 on v6

--- a/solution.py
+++ b/solution.py
@@ -15,7 +15,7 @@
 OFFS = (1, 2, 3, 4, 127, 126, 125, 124, 64)
 BACK = (4, 5, 6, 7, 0, 1, 2, 3, 8)
 LANES = len(OFFS)
-LANE_ORDER = (8, 3, 7, 2, 6, 1, 5, 0, 4)
+LANE_ORDER = (3, 7, 2, 6, 8, 1, 5, 0, 4)
 ROWS = 16 * LANES
 TOTAL_CELLS = float(N * O * C)
 COUPLING = 0.25
@@ -400,6 +400,8 @@
         chosen = dot(os_ref[...], parts[0]) + dot(os_ref[...], parts[1])
         copies = face_copies(slot)
         for copy in copies:
+            copy.wait_send()
+        for copy in copies:
             copy.wait_recv()
         got = face_got[slot]
         wide = jnp.concatenate([got] * 3, axis=1) * smask_ref[0]
@@ -410,8 +412,6 @@
         chosen = chosen * (1.0 / 6.0)
         if shift is not None:
             chosen = chosen + shift()
-        for copy in copies:
-            copy.wait_send()
         send_faces(chosen, later_slot)
         raw = away_ghosts(got)
         total = total + (placed(raw, 0) + placed(raw, 1) + placed(raw, 2))

time: 66.1 us -> 65.8 us (level)
  no operation moved by 1% of the time
where the time goes in v7:
time: 65.8 us; the launch traced here: 65.3 us
  Pallas kernels  60.9 us (93%)
  local copies, waits for them, and re-layouts  3.68 us (6%)
  between operations  0.69 us (1%)
    pallas_call x1, Pallas kernels, on_device(): pl.pallas_call(kernel, out_shape=(jax.ShapeDtypeStruct((O, C), f32), jax....  60.9 us
    unnamed x16, local copies, waits for them, and re-layouts  3.68 us

profile of v7, /device:TPU:1, one launch (start us, length us, event | category | flops | bytes accessed | tf_op | source)
XLA Modules:
  0.0 65.3 jit_solution(10540213731486752693)
XLA Ops:
  0.6 0.0 copy-start.3
  0.6 0.0 copy-start.2
  0.7 0.0 copy-start.1
  0.7 0.0 copy-start.5
  0.7 0.0 copy-start.6
  0.7 0.6 copy-done.3
  1.3 0.0 copy-done.2
  1.3 0.0 copy-done.1
  1.4 0.0 copy-done.5
  1.4 0.0 copy-done.6
  1.4 0.0 copy-start
  1.4 0.9 %copy-done = f32[128,256]{1,0:T(8,128)S(1)} copy-done((f32[128,256]{1,0:T(8,128)S(1)}, f32[128,256]{1,0:T(8,128)}, u32[]{:S(2)}) %copy-start) | copy-done | bytes 131096
  2.3 0.0 copy-start.4
  2.3 0.7 %copy-done.4 = s32[64,6,1]{0,2,1:T(1,128)S(1)} copy-done((s32[64,6,1]{0,2,1:T(1,128)S(1)}, s32[64,6,1]{0,2,1:T(1,128)}, u32[]{:S(2)}) %copy-start.4) | copy-done | bytes 1560
  2.9 60.9 %shard_map.95 = (f32[64,512]{1,0:T(8,128)S(1)}, f32[3,128,256]{2,1,0:T(8,128)S(1)}) custom-call(f32[3,128,256]{2,1,0:T(8,128)} %bitcast.15, f32[128,256]{1,0:T(8,128)S(1)} %copy-done, s32[1,128]{1,0:T(1,128)S(1)} %bitcast.13, s32[1,128]{1,0:T(1,128)S(1)} %bitcast.14, s32[6,1,64]{2,1,0:T(1,128)S(1)} %bitcast.12, s32[6,64]{1,0:T(8,128)S(1)} %bitcast.9, ...), custom_call_target="tpu_custom_call" | custom-call | tf_op jit(solution)/shard_map/pallas_call | solution.py:537
  63.9 0.7 %copy.12 = f32[64,512]{1,0:T(8,128)} copy(f32[64,512]{1,0:T(8,128)S(1)} %get-tuple-element.8) | data formatting | bytes 262144
  64.6 0.7 %copy.13 = f32[128,3,256]{2,0,1:T(8,128)} copy(f32[128,3,256]{2,0,1:T(8,128)S(1)} %bitcast.8) | data formatting | bytes 786432
Async XLA Ops:
  0.6 0.7 %copy-start.3 = (s32[64,6]{0,1:T(8,128)S(1)}, s32[64,6]{0,1:T(8,128)}, u32[]{:S(2)}) copy-start(s32[64,6]{0,1:T(8,128)} %param.15) | copy-start | bytes 4612
  0.6 0.7 %copy-start.2 = (s32[64,6]{0,1:T(8,128)S(1)}, s32[64,6]{0,1:T(8,128)}, u32[]{:S(2)}) copy-start(s32[64,6]{0,1:T(8,128)} %param.14) | copy-start | bytes 4612
  0.7 0.7 %copy-start.1 = (s32[64,6]{0,1:T(8,128)S(1)}, s32[64,6]{0,1:T(8,128)}, u32[]{:S(2)}) copy-start(s32[64,6]{0,1:T(8,128)} %param.13) | copy-start | bytes 4612
  0.7 0.7 %copy-start.5 = (s32[128,1]{0,1:T(1,128)S(1)}, s32[128,1]{0,1:T(1,128)}, u32[]{:S(2)}) copy-start(s32[128,1]{0,1:T(1,128)} %param.10) | copy-start | bytes 1540
  0.7 0.7 %copy-start.6 = (s32[128]{0:T(128)S(1)}, s32[128]{0:T(128)}, u32[]{:S(2)}) copy-start(s32[128]{0:T(128)} %param.11) | copy-start | bytes 1540
  1.4 0.9 %copy-start = (f32[128,256]{1,0:T(8,128)S(1)}, f32[128,256]{1,0:T(8,128)}, u32[]{:S(2)}) copy-start(f32[128,256]{1,0:T(8,128)} %mass_hbm.1) | copy-start | bytes 393220
  2.3 0.7 %copy-start.4 = (s32[64,6,1]{0,2,1:T(1,128)S(1)}, s32[64,6,1]{0,2,1:T(1,128)}, u32[]{:S(2)}) copy-start(s32[64,6,1]{0,2,1:T(1,128)} %param.12) | copy-start | bytes 4612
